TPU v7x, 256 devices: a whole 4x4x8 slice. The times are simulated.
256 devices in a mesh: clip: 128 (over z, y, x), row: 2 (over core).
Axes of the slice: x: 4, y: 4, z: 8, core: 2. Of those that a mesh axis runs over, the one named last changes fastest.
Arguments:
- queries: bfloat16 [128, 512, 1792], P('clip', 'row'), may hold values from -36 to 36
- frames_kv: bfloat16 [128, 512, 512], P('clip', 'row'), may hold values from -20 to 20
- summary_kv: bfloat16 [128, 32, 512], P('clip', 'row'), may hold values from -6 to 6
- lengths: int32 [128], P('clip'), may hold values from 128 to 512, as said below
- caps: int32 [128], P('clip'), may hold values from 8 to 32, as said below
Outputs:
- attended: bfloat16 [128, 512, 1792], P('clip', 'row')
Inputs may be any that keep to these rules, and one draw needn't show every extreme that they name: `lengths`: some clip of every draw has 512 frame tokens. `caps`: some clip of every draw keeps 32 summary tokens.
All inputs are finite; a program needn't handle non-finite values.
Results may differ from a plain program's by a relative error of at most 0.01.
Values may be sent and summed in bfloat16 or wider, within the bound.
No kernel may reach another device: no remote copies, remote signals or barrier semaphores. Data moves between devices by JAX's collectives and lax.ppermute only.
A program may use at most 64 MiB of HBM per device.

v0:
```python
import math

import jax
import jax.numpy as jnp
from jax import lax
from jax.sharding import Mesh
from jax.sharding import PartitionSpec as P

KVH = 2
HD = 128
WINDOW = 128
CLIP = ("clip_0", "clip_1", "clip_2")


masked_score = -1e30


def passed_along(block, axis, distance):
    devices = range(lax.axis_size(axis))
    route = [(i - distance, i) for i in devices if i - distance in devices]
    return lax.ppermute(block, axis, route)


def gather_axes(array, axes, dim):
    if not axes:
        return array
    nearer = lax.all_gather(array, axes[-1], axis=dim, tiled=True)
    return gather_axes(nearer, axes[:-1], dim)


def attend(state, query_heads, keys, values, valid):
    largest, total, accum = state
    scores = jnp.einsum(
        "tkgd,skd->kgts", query_heads, keys, preferred_element_type=jnp.float32
    ) * HD ** (-0.5)
    masked = jnp.where(valid, scores, masked_score)
    fresh = jnp.maximum(largest, jnp.max(masked, axis=-1))
    weights = jnp.where(valid, jnp.exp(masked - fresh[..., None]), 0.0)
    factor = jnp.exp(largest - fresh)
    total = total * factor + jnp.sum(weights, axis=-1)
    accum = accum * factor[..., None] + jnp.einsum(
        "kgts,skd->kgtd", weights.astype(jnp.bfloat16), values, preferred_element_type=jnp.float32
    )
    return (fresh, total, accum)


def split_rows(kv_rows):
    count = kv_rows.shape[0]
    keys = kv_rows[:, : KVH * HD].reshape(count, KVH, HD)
    values = kv_rows[:, KVH * HD :].reshape(count, KVH, HD)
    return (keys, values)


def fold_summary(state, piece, query_heads, clip_index):
    rows_kv, clip_caps = piece
    clip_count = rows_kv.shape[0]
    slot_count = rows_kv.shape[1]
    flat = rows_kv.reshape(clip_count * slot_count, rows_kv.shape[2])
    clip_ids = jnp.arange(clip_count)
    live = (jnp.arange(slot_count)[None, :] < clip_caps[:, None]) & (clip_ids[:, None] < clip_index)
    live = live.reshape(-1)
    count = clip_count * slot_count
    block = math.gcd(count, 512)
    blocks_kv = flat.reshape(count // block, block, flat.shape[1])
    blocks_live = live.reshape(count // block, block)

    def step_block(carry, item):
        kv_block, live_block = item
        keys, values = split_rows(kv_block)
        return (attend(carry, query_heads, keys, values, live_block), None)

    state, unused = lax.scan(step_block, state, (blocks_kv, blocks_live))
    return state


def shards(queries, frames_kv, summary_kv, lengths, caps):
    tokens_here = queries.shape[1]
    group = queries.shape[2] // (KVH * HD)
    row_index = lax.axis_index("row")
    clip_index = lax.axis_index(CLIP)
    own_heads = queries[0].reshape(tokens_here, KVH, group, HD)
    frames = frames_kv[0]
    rim = passed_along(frames[tokens_here - WINDOW :], "row", 1)
    local_kv = jnp.concatenate([rim, frames], axis=0)
    query_pos = row_index * tokens_here + jnp.arange(tokens_here)
    key_pos = row_index * tokens_here - WINDOW + jnp.arange(WINDOW + tokens_here)
    near = (
        (key_pos[None, :] >= 0)
        & (key_pos[None, :] <= query_pos[:, None])
        & (key_pos[None, :] > query_pos[:, None] - WINDOW)
    )
    start_state = (
        jnp.full((KVH, group, tokens_here), masked_score, jnp.float32),
        jnp.zeros((KVH, group, tokens_here), jnp.float32),
        jnp.zeros((KVH, group, tokens_here, HD), jnp.float32),
    )
    local_keys, local_values = split_rows(local_kv)
    state = attend(start_state, own_heads, local_keys, local_values, near)
    slots = lax.all_gather(summary_kv, "row", axis=1, tiled=True)
    state = fold_summary(
        state, (gather_axes(slots, CLIP, 0), gather_axes(caps, CLIP, 0)), own_heads, clip_index
    )
    largest, total, accum = state
    result = accum / total[..., None]
    result = jnp.transpose(result, (2, 0, 1, 3)).reshape(tokens_here, KVH * group * HD)
    result = jnp.where((query_pos < lengths[0])[:, None], result, 0.0)
    return result.astype(jnp.bfloat16)[None]


def solution(mesh):
    torus = Mesh(
        mesh.devices.reshape(8, 4, 4, mesh.shape["row"]), ("clip_0", "clip_1", "clip_2", "row")
    )
    placed = (P(CLIP, "row", None), P(CLIP, "row", None), P(CLIP, "row", None), P(CLIP), P(CLIP))
    return jax.shard_map(
        shards, mesh=torus, in_specs=placed, out_specs=P(CLIP, "row", None), check_vma=False
    )
```

profile of v0, /device:TPU:1, one launch (start us, length us, event | category | flops | bytes accessed | tf_op | source)
XLA Modules:
  0.0 180.5 jit_solution(5718618525549545784)
XLA Ops:
  6.5 4.9 %all_gather.24 = bf16[1,32,512]{2,1,0:T(8,128)(2,1)S(1)} all-gather(bf16[1,16,512]{2,1,0:T(8,128)(2,1)} %param.9), channel_id=1, replica_groups=mesh['clip_0'=8,'clip_1'=4,'clip_2'=4,'row'=2] {'row'}, dimensions={1}, use_global_device_ids=true | all-gather | bytes 49152 | tf_op jit(solution)/shard_map/all_gather | solution.py:99
  11.5 9.1 %all_gather.25 = bf16[4,32,512]{2,1,0:T(8,128)(2,1)S(1)} all-gather(bf16[1,32,512]{2,1,0:T(8,128)(2,1)S(1)} %all_gather.24), channel_id=1, replica_groups=mesh['clip_0'=8,'clip_1'=4,'clip_2'=4,'row'=2] {'clip_2'}, dimensions={0}, use_global_device_ids=true | all-gather | bytes 163840 | tf_op jit(solution)/shard_map/all_gather | solution.py:27
  20.6 10.6 %all_gather.26 = bf16[16,32,512]{2,1,0:T(8,128)(2,1)} all-gather(bf16[4,32,512]{2,1,0:T(8,128)(2,1)S(1)} %all_gather.25), channel_id=1, replica_groups=mesh['clip_0'=8,'clip_1'=4,'clip_2'=4,'row'=2] {'clip_1'}, dimensions={0}, use_global_device_ids=true | all-gather | bytes 655360 | tf_op jit(solution)/shard_map/all_gather | solution.py:27
  31.9 1.1 copy.39
  33.0 1.3 dynamic-slice
  34.2 0.7 dynamic-update-slice
  35.0 1.3 collective-permute-start
  36.3 5.3 %all-reduce = s32[4]{0:T(128)S(1)} all-reduce(s32[4]{0:T(128)S(1)} %dynamic-update-slice), channel_id=1, replica_groups=mesh['clip_0'=8,'clip_1'=4,'clip_2'=4,'row'=2] {'clip_2'}, use_global_device_ids=true, to_apply=%add | all-reduce | flops 4 | bytes 32
  41.6 1.3 dynamic-slice.2
  42.9 1.3 dynamic-slice.1
  45.4 0.2 dynamic-update-slice.1
  45.7 7.2 %all-reduce.1 = s32[16]{0:T(128)S(1)} all-reduce(s32[16]{0:T(128)S(1)} %dynamic-update-slice.1), channel_id=1, replica_groups=mesh['clip_0'=8,'clip_1'=4,'clip_2'=4,'row'=2] {'clip_1'}, use_global_device_ids=true, to_apply=%add.1 | all-reduce | flops 16 | bytes 128
  53.1 14.6 %all-reduce.2 = s32[128]{0:T(128)S(1)} all-reduce(s32[128]{0:T(128)S(1)} %dynamic-update-slice.2), channel_id=1, replica_groups=mesh['clip_0'=8,'clip_1'=4,'clip_2'=4,'row'=2] {'clip_0'}, use_global_device_ids=true, to_apply=%add.2 | all-reduce | flops 128 | bytes 1024
  69.1 1.5 copy.41
  70.6 0.6 copy.47
  71.3 1.1 fusion.13
  72.4 1.3 fusion.15
  73.8 3.1 %fusion.19 = f32[2,7,256,128]{3,2,1,0:T(8,128)} fusion(bf16[384,2,128,1]{0,2,3,1:T(8,128)(2,1)S(1)} %bitcast.94, f32[2,384,256,7]{2,1,3,0:T(8,128)S(1)} %get-tuple-element.91, f32[2,7,256]{2,1,0:T(8,128)S(1)} %broadcast_maximum_fusion, pred[256,384]{0,1:T(8,128)(4,1)S(1)} %compare_and_fusion, f32[2,7,256]{2,1,0:T(8,128)S(1)} %get-tuple-element.88), kind=kOutput, calls=%fused_computation.26 | convolution fusion | flops 359661568 | bytes 7663616 | tf_op jit(solution)/shard_map/kgts,skd->kgtd/dot_general | solution.py:41
  76.8 15.8 %all-gather.2.cloned.1.call-done = bf16[128,32,512]{2,1,0:T(8,128)(2,1)} async-done(((bf16[16,32,512]{2,1,0:T(8,128)(2,1)}), bf16[128,32,512]{2,1,0:T(8,128)(2,1)}) %all-gather.2.cloned.1.call-update) | async-done | bytes 4194320 | tf_op jit(solution)/shard_map/all_gather | solution.py:27
  92.6 77.4 %while.14 = (s32[]{:T(128)}, f32[2,7,256]{2,1,0:T(8,128)S(1)}, f32[2,7,256]{2,1,0:T(8,128)S(1)}, f32[2,7,256,128]{3,2,1,0:T(8,128)}, pred[8,512]{1,0:T(8,128)(4,...) while((s32[]{:T(128)}, f32[2,7,256]{2,1,0:T(8,128)S(1)}, ...), condition=%wide.region_5.6_spmd, body=%wide.region_2.5_spmd.sunk | while | flops 964303872 | bytes 45189788 | solution.py:72
  92.7 1.1 constant_dynamic-slice_fusion.2
  93.7 0.2 copy.67
  94.0 1.8 %bitcast_reduce_fusion.2 = (f32[2,7,256]{2,1,0:T(8,128)S(1)}, f32[2,512,256,7]{2,1,3,0:T(8,128)S(1)}) fusion(pred[512]{0:T(512)(128)(4,1)S(1)} %dynamic-slice_reduce_fusion.2, bf16[512,2,128,1]{0,2,3,1:T(8,128)(2,1)S(1)} %bitcast.86, bf16[256,2,7,128]{3,0,2,1:T(8,128)(2,1)S(1)} %get-tuple-element.171), kind=kOutput, calls=%fused_computation.1.clone.1 | convolution fusion | flops 475263488 | bytes 8534528 | tf_op jit(solution)/shard_map/while/body/eval_jaxpr/tkgd,skd->kgts/dot_general | solution.py:33
  95.9 2.1 %fusion.47 = f32[2,7,256]{2,1,0:T(8,128)S(1)} fusion(f32[2,512,256,7]{2,1,3,0:T(8,128)S(1)} %get-tuple-element.145, f32[2,7,256]{2,1,0:T(8,128)S(1)} %max.4, pred[512]{0:T(512)(128)(4,1)S(1)} %dynamic-slice_reduce_fusion.2), kind=kLoop, calls=%fused_computation.6.clone.1 | loop fusion | flops 9171456 | bytes 7369216 | tf_op jit(solution)/shard_map/while/body/eval_jaxpr/reduce_sum | solution.py:40
  98.0 3.1 %multiply_add_fusion.5 = f32[2,7,256,128]{3,2,1,0:T(8,128)S(1)} fusion(f32[2,7,256,128]{3,2,1,0:T(8,128)S(1)} %copy-done, bf16[512,2,128,1]{0,2,3,1:T(8,128)(2,1)S(1)} %bitcast.89, f32[2,512,256,7]{2,1,3,0:T(8,128)S(1)} %get-tuple-element.145, f32[2,7,256]{2,1,0:T(8,128)S(1)} %max.4, pred[512]{0:T(512)(128)(4,1)S(1)} %dynamic-slice_reduce_fusion.2, ...), kind=kOutput, calls=%fused_computation.10.clone.1 | convolution fusion | flops 479854592 | bytes 11301376 | tf_op jit(solution)/shard_map/while/body/eval_jaxpr/kgts,skd->kgtd/dot_general | solution.py:41
  101.1 1.2 copy-done.1
  102.3 1.1 constant_dynamic-slice_fusion.2
  103.7 1.8 %bitcast_reduce_fusion.2 = (f32[2,7,256]{2,1,0:T(8,128)S(1)}, f32[2,512,256,7]{2,1,3,0:T(8,128)S(1)}) fusion(pred[512]{0:T(512)(128)(4,1)S(1)} %dynamic-slice_reduce_fusion.2, bf16[512,2,128,1]{0,2,3,1:T(8,128)(2,1)S(1)} %bitcast.86, bf16[256,2,7,128]{3,0,2,1:T(8,128)(2,1)S(1)} %get-tuple-element.171), kind=kOutput, calls=%fused_computation.1.clone.1 | convolution fusion | flops 475263488 | bytes 8534528 | tf_op jit(solution)/shard_map/while/body/eval_jaxpr/tkgd,skd->kgts/dot_general | solution.py:33
  105.6 2.1 %fusion.47 = f32[2,7,256]{2,1,0:T(8,128)S(1)} fusion(f32[2,512,256,7]{2,1,3,0:T(8,128)S(1)} %get-tuple-element.145, f32[2,7,256]{2,1,0:T(8,128)S(1)} %max.4, pred[512]{0:T(512)(128)(4,1)S(1)} %dynamic-slice_reduce_fusion.2), kind=kLoop, calls=%fused_computation.6.clone.1 | loop fusion | flops 9171456 | bytes 7369216 | tf_op jit(solution)/shard_map/while/body/eval_jaxpr/reduce_sum | solution.py:40
  107.7 3.1 %multiply_add_fusion.5 = f32[2,7,256,128]{3,2,1,0:T(8,128)S(1)} fusion(f32[2,7,256,128]{3,2,1,0:T(8,128)S(1)} %copy-done, bf16[512,2,128,1]{0,2,3,1:T(8,128)(2,1)S(1)} %bitcast.89, f32[2,512,256,7]{2,1,3,0:T(8,128)S(1)} %get-tuple-element.145, f32[2,7,256]{2,1,0:T(8,128)S(1)} %max.4, pred[512]{0:T(512)(128)(4,1)S(1)} %dynamic-slice_reduce_fusion.2, ...), kind=kOutput, calls=%fused_computation.10.clone.1 | convolution fusion | flops 479854592 | bytes 11301376 | tf_op jit(solution)/shard_map/while/body/eval_jaxpr/kgts,skd->kgtd/dot_general | solution.py:41
  110.7 1.2 copy-done.1
  112.0 1.1 constant_dynamic-slice_fusion.2
  113.1 0.2 copy.67
  113.4 1.8 %bitcast_reduce_fusion.2 = (f32[2,7,256]{2,1,0:T(8,128)S(1)}, f32[2,512,256,7]{2,1,3,0:T(8,128)S(1)}) fusion(pred[512]{0:T(512)(128)(4,1)S(1)} %dynamic-slice_reduce_fusion.2, bf16[512,2,128,1]{0,2,3,1:T(8,128)(2,1)S(1)} %bitcast.86, bf16[256,2,7,128]{3,0,2,1:T(8,128)(2,1)S(1)} %get-tuple-element.171), kind=kOutput, calls=%fused_computation.1.clone.1 | convolution fusion | flops 475263488 | bytes 8534528 | tf_op jit(solution)/shard_map/while/body/eval_jaxpr/tkgd,skd->kgts/dot_general | solution.py:33
  115.2 2.1 %fusion.47 = f32[2,7,256]{2,1,0:T(8,128)S(1)} fusion(f32[2,512,256,7]{2,1,3,0:T(8,128)S(1)} %get-tuple-element.145, f32[2,7,256]{2,1,0:T(8,128)S(1)} %max.4, pred[512]{0:T(512)(128)(4,1)S(1)} %dynamic-slice_reduce_fusion.2), kind=kLoop, calls=%fused_computation.6.clone.1 | loop fusion | flops 9171456 | bytes 7369216 | tf_op jit(solution)/shard_map/while/body/eval_jaxpr/reduce_sum | solution.py:40
  117.3 3.1 %multiply_add_fusion.5 = f32[2,7,256,128]{3,2,1,0:T(8,128)S(1)} fusion(f32[2,7,256,128]{3,2,1,0:T(8,128)S(1)} %copy-done, bf16[512,2,128,1]{0,2,3,1:T(8,128)(2,1)S(1)} %bitcast.89, f32[2,512,256,7]{2,1,3,0:T(8,128)S(1)} %get-tuple-element.145, f32[2,7,256]{2,1,0:T(8,128)S(1)} %max.4, pred[512]{0:T(512)(128)(4,1)S(1)} %dynamic-slice_reduce_fusion.2, ...), kind=kOutput, calls=%fused_computation.10.clone.1 | convolution fusion | flops 479854592 | bytes 11301376 | tf_op jit(solution)/shard_map/while/body/eval_jaxpr/kgts,skd->kgtd/dot_general | solution.py:41
  120.4 1.2 copy-done.1
  121.7 1.1 constant_dynamic-slice_fusion.2
  123.0 1.8 %bitcast_reduce_fusion.2 = (f32[2,7,256]{2,1,0:T(8,128)S(1)}, f32[2,512,256,7]{2,1,3,0:T(8,128)S(1)}) fusion(pred[512]{0:T(512)(128)(4,1)S(1)} %dynamic-slice_reduce_fusion.2, bf16[512,2,128,1]{0,2,3,1:T(8,128)(2,1)S(1)} %bitcast.86, bf16[256,2,7,128]{3,0,2,1:T(8,128)(2,1)S(1)} %get-tuple-element.171), kind=kOutput, calls=%fused_computation.1.clone.1 | convolution fusion | flops 475263488 | bytes 8534528 | tf_op jit(solution)/shard_map/while/body/eval_jaxpr/tkgd,skd->kgts/dot_general | solution.py:33
  124.9 2.1 %fusion.47 = f32[2,7,256]{2,1,0:T(8,128)S(1)} fusion(f32[2,512,256,7]{2,1,3,0:T(8,128)S(1)} %get-tuple-element.145, f32[2,7,256]{2,1,0:T(8,128)S(1)} %max.4, pred[512]{0:T(512)(128)(4,1)S(1)} %dynamic-slice_reduce_fusion.2), kind=kLoop, calls=%fused_computation.6.clone.1 | loop fusion | flops 9171456 | bytes 7369216 | tf_op jit(solution)/shard_map/while/body/eval_jaxpr/reduce_sum | solution.py:40
  127.0 3.1 %multiply_add_fusion.5 = f32[2,7,256,128]{3,2,1,0:T(8,128)S(1)} fusion(f32[2,7,256,128]{3,2,1,0:T(8,128)S(1)} %copy-done, bf16[512,2,128,1]{0,2,3,1:T(8,128)(2,1)S(1)} %bitcast.89, f32[2,512,256,7]{2,1,3,0:T(8,128)S(1)} %get-tuple-element.145, f32[2,7,256]{2,1,0:T(8,128)S(1)} %max.4, pred[512]{0:T(512)(128)(4,1)S(1)} %dynamic-slice_reduce_fusion.2, ...), kind=kOutput, calls=%fused_computation.10.clone.1 | convolution fusion | flops 479854592 | bytes 11301376 | tf_op jit(solution)/shard_map/while/body/eval_jaxpr/kgts,skd->kgtd/dot_general | solution.py:41
  130.1 1.2 copy-done.1
  131.4 1.1 constant_dynamic-slice_fusion.2
  132.7 1.8 %bitcast_reduce_fusion.2 = (f32[2,7,256]{2,1,0:T(8,128)S(1)}, f32[2,512,256,7]{2,1,3,0:T(8,128)S(1)}) fusion(pred[512]{0:T(512)(128)(4,1)S(1)} %dynamic-slice_reduce_fusion.2, bf16[512,2,128,1]{0,2,3,1:T(8,128)(2,1)S(1)} %bitcast.86, bf16[256,2,7,128]{3,0,2,1:T(8,128)(2,1)S(1)} %get-tuple-element.171), kind=kOutput, calls=%fused_computation.1.clone.1 | convolution fusion | flops 475263488 | bytes 8534528 | tf_op jit(solution)/shard_map/while/body/eval_jaxpr/tkgd,skd->kgts/dot_general | solution.py:33
  134.6 2.1 %fusion.47 = f32[2,7,256]{2,1,0:T(8,128)S(1)} fusion(f32[2,512,256,7]{2,1,3,0:T(8,128)S(1)} %get-tuple-element.145, f32[2,7,256]{2,1,0:T(8,128)S(1)} %max.4, pred[512]{0:T(512)(128)(4,1)S(1)} %dynamic-slice_reduce_fusion.2), kind=kLoop, calls=%fused_computation.6.clone.1 | loop fusion | flops 9171456 | bytes 7369216 | tf_op jit(solution)/shard_map/while/body/eval_jaxpr/reduce_sum | solution.py:40
  136.7 3.1 %multiply_add_fusion.5 = f32[2,7,256,128]{3,2,1,0:T(8,128)S(1)} fusion(f32[2,7,256,128]{3,2,1,0:T(8,128)S(1)} %copy-done, bf16[512,2,128,1]{0,2,3,1:T(8,128)(2,1)S(1)} %bitcast.89, f32[2,512,256,7]{2,1,3,0:T(8,128)S(1)} %get-tuple-element.145, f32[2,7,256]{2,1,0:T(8,128)S(1)} %max.4, pred[512]{0:T(512)(128)(4,1)S(1)} %dynamic-slice_reduce_fusion.2, ...), kind=kOutput, calls=%fused_computation.10.clone.1 | convolution fusion | flops 479854592 | bytes 11301376 | tf_op jit(solution)/shard_map/while/body/eval_jaxpr/kgts,skd->kgtd/dot_general | solution.py:41
  139.8 1.2 copy-done.1
  141.1 1.1 constant_dynamic-slice_fusion.2
  142.4 1.8 %bitcast_reduce_fusion.2 = (f32[2,7,256]{2,1,0:T(8,128)S(1)}, f32[2,512,256,7]{2,1,3,0:T(8,128)S(1)}) fusion(pred[512]{0:T(512)(128)(4,1)S(1)} %dynamic-slice_reduce_fusion.2, bf16[512,2,128,1]{0,2,3,1:T(8,128)(2,1)S(1)} %bitcast.86, bf16[256,2,7,128]{3,0,2,1:T(8,128)(2,1)S(1)} %get-tuple-element.171), kind=kOutput, calls=%fused_computation.1.clone.1 | convolution fusion | flops 475263488 | bytes 8534528 | tf_op jit(solution)/shard_map/while/body/eval_jaxpr/tkgd,skd->kgts/dot_general | solution.py:33
  144.3 2.1 %fusion.47 = f32[2,7,256]{2,1,0:T(8,128)S(1)} fusion(f32[2,512,256,7]{2,1,3,0:T(8,128)S(1)} %get-tuple-element.145, f32[2,7,256]{2,1,0:T(8,128)S(1)} %max.4, pred[512]{0:T(512)(128)(4,1)S(1)} %dynamic-slice_reduce_fusion.2), kind=kLoop, calls=%fused_computation.6.clone.1 | loop fusion | flops 9171456 | bytes 7369216 | tf_op jit(solution)/shard_map/while/body/eval_jaxpr/reduce_sum | solution.py:40
  146.4 3.1 %multiply_add_fusion.5 = f32[2,7,256,128]{3,2,1,0:T(8,128)S(1)} fusion(f32[2,7,256,128]{3,2,1,0:T(8,128)S(1)} %copy-done, bf16[512,2,128,1]{0,2,3,1:T(8,128)(2,1)S(1)} %bitcast.89, f32[2,512,256,7]{2,1,3,0:T(8,128)S(1)} %get-tuple-element.145, f32[2,7,256]{2,1,0:T(8,128)S(1)} %max.4, pred[512]{0:T(512)(128)(4,1)S(1)} %dynamic-slice_reduce_fusion.2, ...), kind=kOutput, calls=%fused_computation.10.clone.1 | convolution fusion | flops 479854592 | bytes 11301376 | tf_op jit(solution)/shard_map/while/body/eval_jaxpr/kgts,skd->kgtd/dot_general | solution.py:41
  149.5 1.2 copy-done.1
  150.7 1.1 constant_dynamic-slice_fusion.2
  152.1 1.8 %bitcast_reduce_fusion.2 = (f32[2,7,256]{2,1,0:T(8,128)S(1)}, f32[2,512,256,7]{2,1,3,0:T(8,128)S(1)}) fusion(pred[512]{0:T(512)(128)(4,1)S(1)} %dynamic-slice_reduce_fusion.2, bf16[512,2,128,1]{0,2,3,1:T(8,128)(2,1)S(1)} %bitcast.86, bf16[256,2,7,128]{3,0,2,1:T(8,128)(2,1)S(1)} %get-tuple-element.171), kind=kOutput, calls=%fused_computation.1.clone.1 | convolution fusion | flops 475263488 | bytes 8534528 | tf_op jit(solution)/shard_map/while/body/eval_jaxpr/tkgd,skd->kgts/dot_general | solution.py:33
  154.0 2.1 %fusion.47 = f32[2,7,256]{2,1,0:T(8,128)S(1)} fusion(f32[2,512,256,7]{2,1,3,0:T(8,128)S(1)} %get-tuple-element.145, f32[2,7,256]{2,1,0:T(8,128)S(1)} %max.4, pred[512]{0:T(512)(128)(4,1)S(1)} %dynamic-slice_reduce_fusion.2), kind=kLoop, calls=%fused_computation.6.clone.1 | loop fusion | flops 9171456 | bytes 7369216 | tf_op jit(solution)/shard_map/while/body/eval_jaxpr/reduce_sum | solution.py:40
  156.1 3.1 %multiply_add_fusion.5 = f32[2,7,256,128]{3,2,1,0:T(8,128)S(1)} fusion(f32[2,7,256,128]{3,2,1,0:T(8,128)S(1)} %copy-done, bf16[512,2,128,1]{0,2,3,1:T(8,128)(2,1)S(1)} %bitcast.89, f32[2,512,256,7]{2,1,3,0:T(8,128)S(1)} %get-tuple-element.145, f32[2,7,256]{2,1,0:T(8,128)S(1)} %max.4, pred[512]{0:T(512)(128)(4,1)S(1)} %dynamic-slice_reduce_fusion.2, ...), kind=kOutput, calls=%fused_computation.10.clone.1 | convolution fusion | flops 479854592 | bytes 11301376 | tf_op jit(solution)/shard_map/while/body/eval_jaxpr/kgts,skd->kgtd/dot_general | solution.py:41
  159.2 1.2 copy-done.1
  160.4 1.1 constant_dynamic-slice_fusion.2
  161.8 1.8 %bitcast_reduce_fusion.2 = (f32[2,7,256]{2,1,0:T(8,128)S(1)}, f32[2,512,256,7]{2,1,3,0:T(8,128)S(1)}) fusion(pred[512]{0:T(512)(128)(4,1)S(1)} %dynamic-slice_reduce_fusion.2, bf16[512,2,128,1]{0,2,3,1:T(8,128)(2,1)S(1)} %bitcast.86, bf16[256,2,7,128]{3,0,2,1:T(8,128)(2,1)S(1)} %get-tuple-element.171), kind=kOutput, calls=%fused_computation.1.clone.1 | convolution fusion | flops 475263488 | bytes 8534528 | tf_op jit(solution)/shard_map/while/body/eval_jaxpr/tkgd,skd->kgts/dot_general | solution.py:33
  163.6 2.1 %fusion.47 = f32[2,7,256]{2,1,0:T(8,128)S(1)} fusion(f32[2,512,256,7]{2,1,3,0:T(8,128)S(1)} %get-tuple-element.145, f32[2,7,256]{2,1,0:T(8,128)S(1)} %max.4, pred[512]{0:T(512)(128)(4,1)S(1)} %dynamic-slice_reduce_fusion.2), kind=kLoop, calls=%fused_computation.6.clone.1 | loop fusion | flops 9171456 | bytes 7369216 | tf_op jit(solution)/shard_map/while/body/eval_jaxpr/reduce_sum | solution.py:40
  165.7 3.1 %multiply_add_fusion.5 = f32[2,7,256,128]{3,2,1,0:T(8,128)S(1)} fusion(f32[2,7,256,128]{3,2,1,0:T(8,128)S(1)} %copy-done, bf16[512,2,128,1]{0,2,3,1:T(8,128)(2,1)S(1)} %bitcast.89, f32[2,512,256,7]{2,1,3,0:T(8,128)S(1)} %get-tuple-element.145, f32[2,7,256]{2,1,0:T(8,128)S(1)} %max.4, pred[512]{0:T(512)(128)(4,1)S(1)} %dynamic-slice_reduce_fusion.2, ...), kind=kOutput, calls=%fused_computation.10.clone.1 | convolution fusion | flops 479854592 | bytes 11301376 | tf_op jit(solution)/shard_map/while/body/eval_jaxpr/kgts,skd->kgtd/dot_general | solution.py:41
  168.8 1.2 copy-done.1
  170.1 1.8 %copy.48 = f32[2,7,256,128]{2,3,1,0:T(8,128)S(1)} copy(f32[2,7,256,128]{3,2,1,0:T(8,128)} %get-tuple-element.43) | data formatting | bytes 3670016 | tf_op jit(solution)/shard_map/while | solution.py:72
  172.3 1.4 copy.49
  (97 shorter events, 3.4 us)
Async XLA Ops:
  6.5 86.1 %all-gather.2.cloned.1.call-start = ((), (), s32[]{:S(2)}) async-start(), calls=%async_computation | async-start | bytes 4718592 | tf_op jit(solution)/shard_map/all_gather | solution.py:27
  35.0 36.3 %collective-permute-start = (bf16[128,512]{0,1:T(8,128)(2,1)S(1)}, bf16[128,512]{0,1:T(8,128)(2,1)S(1)}, u32[]{:S(2)}, u32[]{:S(2)}) collective-permute-start(bf16[128,512]{0,1:T(8,128)(2,1)S(1)} %slice_bitcast_fusion), channel_id=1, source_target_pairs={{0,1},{2,3},{4,5},{6,7},{8,9},{10,11},{12,13},{14,15},{16,17},{18,... | collective-permute-start | bytes 393224 | tf_op jit(solution)/shard_map/ppermute | solution.py:21
  95.9 2.1 %copy-start = (f32[2,7,256,128]{3,2,1,0:T(8,128)S(1)}, f32[2,7,256,128]{3,2,1,0:T(8,128)}, u32[]{:S(2)}) copy-start(f32[2,7,256,128]{3,2,1,0:T(8,128)} %get-tuple-element.160) | copy-start | bytes 5505028 | tf_op jit(solution)/shard_map/while
  101.1 1.3 copy-start.1
  105.5 2.1 %copy-start = (f32[2,7,256,128]{3,2,1,0:T(8,128)S(1)}, f32[2,7,256,128]{3,2,1,0:T(8,128)}, u32[]{:S(2)}) copy-start(f32[2,7,256,128]{3,2,1,0:T(8,128)} %get-tuple-element.160) | copy-start | bytes 5505028 | tf_op jit(solution)/shard_map/while
  110.7 1.3 copy-start.1
  115.2 2.1 %copy-start = (f32[2,7,256,128]{3,2,1,0:T(8,128)S(1)}, f32[2,7,256,128]{3,2,1,0:T(8,128)}, u32[]{:S(2)}) copy-start(f32[2,7,256,128]{3,2,1,0:T(8,128)} %get-tuple-element.160) | copy-start | bytes 5505028 | tf_op jit(solution)/shard_map/while
  120.4 1.3 copy-start.1
  124.9 2.1 %copy-start = (f32[2,7,256,128]{3,2,1,0:T(8,128)S(1)}, f32[2,7,256,128]{3,2,1,0:T(8,128)}, u32[]{:S(2)}) copy-start(f32[2,7,256,128]{3,2,1,0:T(8,128)} %get-tuple-element.160) | copy-start | bytes 5505028 | tf_op jit(solution)/shard_map/while
  130.1 1.3 copy-start.1
  134.6 2.1 %copy-start = (f32[2,7,256,128]{3,2,1,0:T(8,128)S(1)}, f32[2,7,256,128]{3,2,1,0:T(8,128)}, u32[]{:S(2)}) copy-start(f32[2,7,256,128]{3,2,1,0:T(8,128)} %get-tuple-element.160) | copy-start | bytes 5505028 | tf_op jit(solution)/shard_map/while
  139.8 1.3 copy-start.1
  144.3 2.1 %copy-start = (f32[2,7,256,128]{3,2,1,0:T(8,128)S(1)}, f32[2,7,256,128]{3,2,1,0:T(8,128)}, u32[]{:S(2)}) copy-start(f32[2,7,256,128]{3,2,1,0:T(8,128)} %get-tuple-element.160) | copy-start | bytes 5505028 | tf_op jit(solution)/shard_map/while
  149.4 1.3 copy-start.1
  153.9 2.1 %copy-start = (f32[2,7,256,128]{3,2,1,0:T(8,128)S(1)}, f32[2,7,256,128]{3,2,1,0:T(8,128)}, u32[]{:S(2)}) copy-start(f32[2,7,256,128]{3,2,1,0:T(8,128)} %get-tuple-element.160) | copy-start | bytes 5505028 | tf_op jit(solution)/shard_map/while
  159.1 1.3 copy-start.1
  163.6 2.1 %copy-start = (f32[2,7,256,128]{3,2,1,0:T(8,128)S(1)}, f32[2,7,256,128]{3,2,1,0:T(8,128)}, u32[]{:S(2)}) copy-start(f32[2,7,256,128]{3,2,1,0:T(8,128)} %get-tuple-element.160) | copy-start | bytes 5505028 | tf_op jit(solution)/shard_map/while
  168.8 1.3 copy-start.1
Sparse Core Ops, SparseCore 0:
  31.3 61.2 all-gather.1
where the time goes:
time: 181 us
  blocking collectives  51.8 us (29%)
  matrix products  43.4 us (24%)
  local copies, waits for them, and re-layouts  32.7 us (18%)
  other arithmetic  18.6 us (10%)
  between operations  16.1 us (9%)
  waiting for transfers between devices  15.8 us (9%)
    dot_general x9, matrix products, attend(): jnp.einsum('kgts,skd->kgtd', weights.astype(jnp.bfloat16), values, prefer...  27.6 us
    unnamed x3, blocking collectives  27.2 us
    all_gather x2, blocking collectives, gather_axes(): nearer = lax.all_gather(array, axes[-1], axis=dim, tiled=True)  19.7 us
    reduce_sum x9, other arithmetic, attend(): total = total * factor + jnp.sum(weights, axis=-1)  17.8 us
    dot_general x9, matrix products, attend(): jnp.einsum('tkgd,skd->kgts', query_heads, keys, preferred_element_type=jn...  15.8 us
    all_gather x1, waiting for transfers between devices, gather_axes(): nearer = lax.all_gather(array, axes[-1], axis=dim, tiled=True)  15.8 us
    dynamic_slice x24, local copies, waits for them, and re-layouts, fold_summary(): state, unused = lax.scan(step_block, state, (blocks_kv, blocks_live))  10.5 us
    while x40, local copies, waits for them, and re-layouts  10 us
  transfers between devices with their start and end apart: 2, of which 1 were waited for; matrix products, arithmetic and copies ran while one was open for 8% of the time, Pallas kernels for 0%

commit v1 on v0

v1 whole, which is shorter than its diff:
```python
import functools
import math

import jax
import jax.numpy as jnp
from jax import lax
from jax.experimental import pallas as pl
from jax.experimental.pallas import tpu as pltpu
from jax.sharding import Mesh
from jax.sharding import PartitionSpec as P

KVH = 2
HD = 128
GROUP = 7
WINDOW = 128
CLIP = ("z", "y", "x")
PLANE = ("y", "x", "row")
ZS, YS, XS = 8, 4, 4
TOKENS = 256
HALF = 16
COLUMN = ZS * HALF
RATE = HD**-0.5 * math.log2(math.e)
MARGIN = 250.0
DEAD = 64.0
ALIVE_BELOW = 32.0
CLOSED = -1e30
LARGE = 1e30
DA = (0, 1, 3, 2)
VMEM = pl.BlockSpec(memory_space=pltpu.VMEM)
SMEM = pl.BlockSpec(memory_space=pltpu.SMEM)
NT = (((1,), (1,)), ((), ()))
BQ = 896
BK = 256


def plane_shift(block, phase, distance):
    route = []
    for y in range(YS):
        for x in range(XS):
            for row in range(2):
                if (row == 0) == (phase == 0):
                    to = (y, (x + distance) % XS)
                else:
                    to = ((y + distance) % YS, x)
                route.append(((y * XS + x) * 2 + row, (to[0] * XS + to[1]) * 2 + row))
    return lax.ppermute(block, PLANE, route)


def other_core(block):
    return lax.ppermute(block, "row", [(0, 1), (1, 0)])


def local_kernel(scalars, q_ref, rim_ref, own_ref, qa_ref, acc_ref):
    first_row = scalars[33] == 0
    tile = WINDOW
    t = lax.broadcasted_iota(jnp.int32, (tile, 2 * tile), 0)
    j = lax.broadcasted_iota(jnp.int32, (tile, 2 * tile), 1)
    band = (j > t) & (j <= t + tile)
    low = jnp.where(first_row, tile, 0)
    masks = (band & (j >= low), band)
    lane = lax.broadcasted_iota(jnp.int32, (tile, HD), 1)
    ones = jnp.ones((2 * tile, HD), jnp.bfloat16)
    for h in range(KVH):
        ks = slice(h * HD, (h + 1) * HD)
        vs = slice((KVH + h) * HD, (KVH + h + 1) * HD)
        own_k, own_v = own_ref[:, ks], own_ref[:, vs]
        keys = (jnp.concatenate([rim_ref[:, ks], own_k[:tile]], axis=0), own_k)
        values = (jnp.concatenate([rim_ref[:, vs], own_v[:tile]], axis=0), own_v)
        for g in range(GROUP):
            head = h * GROUP + g
            for part in range(2):
                q = q_ref[part * tile : (part + 1) * tile, head * HD : (head + 1) * HD]
                s = lax.dot_general(q, keys[part], NT, preferred_element_type=jnp.float32)
                top = jnp.max(jnp.where(masks[part], s, CLOSED), axis=1, keepdims=True)
                ref = (top + MARGIN).astype(jnp.bfloat16).astype(jnp.float32)
                p = jnp.where(masks[part], jnp.exp2((s - ref) * RATE), 0.0).astype(jnp.bfloat16)
                value = jnp.concatenate([values[part], ones], axis=1)
                rows = slice(g * TOKENS + part * tile, g * TOKENS + (part + 1) * tile)
                acc_ref[h, rows, :] = jnp.dot(p, value, preferred_element_type=jnp.float32)
                extra = jnp.where(lane == 0, ref, jnp.where(lane == 1, 1.0, 0.0))
                qa_ref[h, rows, :HD] = q
                qa_ref[h, rows, HD:] = extra.astype(jnp.bfloat16)


def build_extra(scalars, chunks, extra):
    row = lax.broadcasted_iota(jnp.int32, (COLUMN, HD), 0)
    lane = lax.broadcasted_iota(jnp.int32, (COLUMN, HD), 1)
    at = 0
    for ref, first in chunks:
        for b in range(ref.shape[0] // COLUMN):
            flag = ref[b * COLUMN : (b + 1) * COLUMN, KVH * HD : KVH * HD + HD].astype(jnp.float32)
            valid = (row < scalars[first + b]) & (flag < ALIVE_BELOW)
            bias = jnp.where(valid, 0.0, CLOSED)
            block = jnp.where(lane == 0, -1.0, jnp.where(lane == 1, bias, 0.0))
            extra[at : at + COLUMN, :] = block.astype(jnp.bfloat16)
            at += COLUMN


def key_tiles(chunks):
    at = 0
    for ref, _ in chunks:
        for b in range(ref.shape[0] // BK):
            yield ref, b * BK, at
            at += BK


def scores(q, ref, start, at, h, extra):
    key = jnp.concatenate([ref[start : start + BK, h * HD : (h + 1) * HD], extra[at : at + BK, :]], axis=1)
    return lax.dot_general(q, key, NT, preferred_element_type=jnp.float32)


def weighted(p, ref, start, h):
    ones = jnp.ones((BK, HD), jnp.bfloat16)
    value = jnp.concatenate([ref[start : start + BK, (KVH + h) * HD : (KVH + h + 1) * HD], ones], axis=1)
    return jnp.dot(p.astype(jnp.bfloat16), value, preferred_element_type=jnp.float32)


def accumulate(acc, q, chunks, h, extra):
    for ref, start, at in key_tiles(chunks):
        p = jnp.exp2(scores(q, ref, start, at, h, extra) * RATE)
        acc = acc + weighted(p, ref, start, h)
    return acc


def remote_kernel(firsts, scalars, qa_ref, acc_ref, *rest):
    refs, (out_ref, extra) = rest[: len(firsts)], rest[len(firsts) :]
    chunks = list(zip(refs, firsts))
    build_extra(scalars, chunks, extra)
    for h in range(KVH):
        def body(i, carry, h=h):
            rows = pl.ds(i * BQ, BQ)
            out_ref[h, rows, :] = accumulate(acc_ref[h, rows, :], qa_ref[h, rows, :], chunks, h, extra)
            return carry
        lax.fori_loop(0, GROUP * TOKENS // BQ, body, 0)


def last_kernel(firsts, new, scalars, qa_ref, local_ref, acc_ref, *rest):
    refs, (out_ref, extra, final) = rest[: len(firsts)], rest[len(firsts) :]
    chunks = list(zip(refs, firsts))
    build_extra(scalars, chunks, extra)
    count = scalars[32]
    token = lax.broadcasted_iota(jnp.int32, (TOKENS, HD), 0)
    for h in range(KVH):
        def body(i, carry, h=h):
            rows = pl.ds(i * BQ, BQ)
            final[rows, :] = accumulate(acc_ref[h, rows, :], qa_ref[h, rows, :], chunks[:new], h, extra)
            return carry
        lax.fori_loop(0, GROUP * TOKENS // BQ, body, 0)

        def too_large():
            return jnp.logical_not(jnp.max(final[:, HD:]) < LARGE)

        @pl.when(too_large())
        def _(h=h):
            def redo(g, carry):
                rows = pl.ds(g * TOKENS, TOKENS)
                q = qa_ref[h, rows, :]
                top = jnp.zeros((TOKENS, 1), jnp.float32)
                for ref, start, at in key_tiles(chunks):
                    s = scores(q, ref, start, at, h, extra)
                    top = jnp.maximum(top, jnp.max(s, axis=1, keepdims=True))
                acc = local_ref[h, rows, :] * jnp.exp2(-top * RATE)
                for ref, start, at in key_tiles(chunks):
                    p = jnp.exp2((scores(q, ref, start, at, h, extra) - top) * RATE)
                    acc = acc + weighted(p, ref, start, h)
                final[rows, :] = acc
                return carry
            lax.fori_loop(0, GROUP, redo, 0)

        for g in range(GROUP):
            rows = slice(g * TOKENS, (g + 1) * TOKENS)
            result = final[rows, :HD] / final[rows, HD:]
            head = h * GROUP + g
            out_ref[:, head * HD : (head + 1) * HD] = jnp.where(token < count, result, 0.0).astype(jnp.bfloat16)


def cost(keys):
    rows = KVH * GROUP * TOKENS
    return pl.CostEstimate(flops=8 * rows * keys * 2 * HD, bytes_accessed=1 << 20, transcendentals=rows * keys)


PARAMS = pltpu.CompilerParams(vmem_limit_bytes=40 * 2**20)
ROWS = GROUP * TOKENS
ACC = jax.ShapeDtypeStruct((KVH, ROWS, 2 * HD), jnp.float32)


def attend_local(scalars, q, rim, own):
    return pl.pallas_call(
        local_kernel,
        out_shape=(jax.ShapeDtypeStruct((KVH, ROWS, 2 * HD), jnp.bfloat16), ACC),
        in_specs=[SMEM] + [VMEM] * 3,
        out_specs=(VMEM, VMEM),
        compiler_params=PARAMS,
        cost_estimate=cost(512),
        name="local",
    )(scalars, q, rim, own)


def attend_remote(scalars, qa, acc, chunks, firsts):
    keys = sum(c.shape[0] for c in chunks)
    return pl.pallas_call(
        functools.partial(remote_kernel, firsts),
        out_shape=ACC,
        in_specs=[SMEM] + [VMEM] * (2 + len(chunks)),
        out_specs=VMEM,
        scratch_shapes=[pltpu.VMEM((keys, HD), jnp.bfloat16)],
        compiler_params=PARAMS,
        cost_estimate=cost(keys),
        name="remote",
    )(scalars, qa, acc, *chunks)


def attend_last(scalars, qa, local, acc, chunks, firsts, new):
    keys = sum(c.shape[0] for c in chunks)
    return pl.pallas_call(
        functools.partial(last_kernel, firsts, new),
        out_shape=jax.ShapeDtypeStruct((TOKENS, KVH * ROWS // TOKENS * HD), jnp.bfloat16),
        in_specs=[SMEM] + [VMEM] * (3 + len(chunks)),
        out_specs=VMEM,
        scratch_shapes=[pltpu.VMEM((keys, HD), jnp.bfloat16), pltpu.VMEM((ROWS, 2 * HD), jnp.float32)],
        compiler_params=PARAMS,
        cost_estimate=cost(keys),
        name="last",
    )(scalars, qa, local, acc, *chunks)


def limits(z, y, x, row):
    db = jnp.repeat(jnp.array((0, 1, 3, 2), jnp.int32), 4)
    da = jnp.tile(jnp.array(DA, jnp.int32), 4)
    found = []
    for role in (row, 1 - row):
        from_y = (y - jnp.where(role == 0, db, da)) % YS
        from_x = (x - jnp.where(role == 0, da, db)) % XS
        before = (from_y * XS + from_x) < (y * XS + x)
        found.append(HALF * (z + before.astype(jnp.int32)))
    return found


def shards(queries, frames_kv, summary_kv, lengths, caps):
    z, y, x, row = (lax.axis_index(name) for name in ("z", "y", "x", "row"))
    own = frames_kv[0]
    rim = lax.ppermute(own[TOKENS - WINDOW :], "row", [(0, 1), (1, 0)])
    scalars = jnp.concatenate(
        limits(z, y, x, row) + [jnp.stack([lengths[0] - row * TOKENS, row]).astype(jnp.int32)]
    )
    slot = lax.broadcasted_iota(jnp.int32, (HALF, 4 * HD), 0) + HALF * row
    entry = lax.broadcasted_iota(jnp.int32, (HALF, 4 * HD), 1)
    mine = jnp.where((slot >= caps[0]) & (entry >= KVH * HD), jnp.bfloat16(DEAD), summary_kv[0])
    copies = jnp.broadcast_to(mine[None], (ZS, HALF, 4 * HD))
    column = lax.all_to_all(copies, "z", 0, 0, tiled=True).reshape(COLUMN, 4 * HD)

    qa, local = attend_local(scalars, queries[0], rim, own)
    near = jnp.concatenate([column] + [plane_shift(column, 0, d) for d in DA[1:]], axis=0)
    half = near.shape[0] // 2
    near_other = other_core(near)
    one = plane_shift(near, 1, 1)
    three = plane_shift(near, 1, 3)
    two_low = plane_shift(one[:half], 1, 1)
    two_high = plane_shift(three[half:], 1, 3)
    one_other, three_other = other_core(one), other_core(three)
    low_other, high_other = other_core(two_low), other_core(two_high)

    acc = attend_remote(scalars, qa, local, (near, near_other), (0, 16))
    acc = attend_remote(scalars, qa, acc, (one, one_other, three, three_other), (4, 20, 8, 24))
    chunks = (two_low, low_other, two_high, high_other)
    chunks += (near, near_other, one, one_other, three, three_other)
    firsts = (12, 28, 14, 30, 0, 16, 4, 20, 8, 24)
    return attend_last(scalars, qa, local, acc, chunks, firsts, 4)[None]


def solution(mesh):
    torus = Mesh(mesh.devices.reshape(ZS, YS, XS, 2), CLIP + ("row",))
    placed = (P(CLIP, "row", None), P(CLIP, "row", None), P(CLIP, "row", None), P(CLIP), P(CLIP))
    return jax.shard_map(
        shards, mesh=torus, in_specs=placed, out_specs=P(CLIP, "row", None), check_vma=False
    )
```

time: 181 us -> 70.4 us (0.39)
  blocking collectives: 51.8 us -> 0 us
  matrix products: 43.4 us -> 0 us
  local copies, waits for them, and re-layouts: 32.7 us -> 4.08 us
  Pallas kernels: 0 us -> 26.4 us
  starting transfers between devices: 1.29 us -> 26.3 us
  other arithmetic: 18.6 us -> 1.74 us
  between operations: 16.1 us -> 1.41 us
  waiting for transfers between devices: 15.8 us -> 10.2 us
    dot_general x18 -> x0, matrix products: 43.4 us -> none  [the longest x9 27.6 us: attend(): jnp.einsum('kgts,skd->kgtd', weights.astype(jnp.bfloat16), values, prefer...]
    unnamed x3 -> x0, blocking collectives: 27.2 us -> none
    pallas_call x0 -> x4, Pallas kernels: none -> 26.4 us  [the longest x2 15.8 us: attend_remote(): pl.pallas_call(functools.partial(remote_kernel, firsts), out_shape=ACC, i...]
    all_gather x3 -> x0, blocking collectives: 24.7 us -> none  [the longest x2 19.7 us: gather_axes(): nearer = lax.all_gather(array, axes[-1], axis=dim, tiled=True)]
    reduce_sum x9 -> x0, other arithmetic: 17.8 us -> none  [attend(): total = total * factor + jnp.sum(weights, axis=-1)]
    ppermute x1 -> x13, starting transfers between devices: 1.29 us -> 17.3 us  [the longest x7 9.87 us: plane_shift(): return lax.ppermute(block, PLANE, route)]
    all_gather x1 -> x0, waiting for transfers between devices: 15.8 us -> none  [gather_axes(): nearer = lax.all_gather(array, axes[-1], axis=dim, tiled=True)]
    while x42 -> x0, local copies, waits for them, and re-layouts: 12.5 us -> none
  transfers between devices with their start and end apart: 2 -> 14, of which waited for: 1 -> 3; matrix products, arithmetic and copies ran while one was open for 8% -> 3% of each run, Pallas kernels for 0% -> 26%
where the time goes in v1:
time: 70.4 us; the launch traced here: 70.1 us
  Pallas kernels  26.4 us (38%)
  starting transfers between devices  26.3 us (37%)
  waiting for transfers between devices  10.2 us (14%)
  local copies, waits for them, and re-layouts  4.08 us (6%)
  other arithmetic  1.74 us (2%)
  between operations  1.41 us (2%)
    pallas_call x2, Pallas kernels, attend_remote(): pl.pallas_call(functools.partial(remote_kernel, firsts), out_shape=ACC, i...  15.8 us
    ppermute x7, starting transfers between devices, plane_shift(): return lax.ppermute(block, PLANE, route)  9.87 us
    all_to_all x1, starting transfers between devices, shards(): lax.all_to_all(copies, 'z', 0, 0, tiled=True).reshape(COLUMN, 4 * HD)  9.01 us
    pallas_call x1, Pallas kernels, attend_last(): pl.pallas_call(functools.partial(last_kernel, firsts, new), out_shape=jax...  8.42 us
    ppermute x5, starting transfers between devices, other_core(): return lax.ppermute(block, 'row', [(0, 1), (1, 0)])  6.4 us
    all_to_all x1, waiting for transfers between devices, shards(): lax.all_to_all(copies, 'z', 0, 0, tiled=True).reshape(COLUMN, 4 * HD)  5.81 us
    ppermute x7, waiting for transfers between devices, plane_shift(): return lax.ppermute(block, PLANE, route)  4.36 us
    pallas_call x1, Pallas kernels, attend_local(): pl.pallas_call(local_kernel, out_shape=(jax.ShapeDtypeStruct((KVH, ROWS,...  2.16 us
  transfers between devices with their start and end apart: 14, of which 3 were waited for; matrix products, arithmetic and copies ran while one was open for 3% of the time, Pallas kernels for 26%

profile of v1, /device:TPU:1, one launch (start us, length us, event | category | flops | bytes accessed | tf_op | source)
XLA Modules:
  0.0 70.1 jit_solution(16812187305446677271)
XLA Ops:
  0.7 0.8 %fusion = bf16[16,512]{1,0:T(8,128)(2,1)S(1)} fusion(bf16[1,16,512]{2,1,0:T(8,128)(2,1)} %param.9, pred[512]{0:T(512)(128)(4,1)S(1)} %iota_compare_fusion, pred[16]{0:T(512)(128)(4,1)S(1)} %add_compare_fusion), kind=kLoop, calls=%fused_computation.3 | loop fusion | flops 16384 | bytes 33296 | tf_op jit(solution)/shard_map/broadcast_in_dim | solution.py:249
  1.5 0.7 broadcast_in_dim.21
  2.1 9.0 %all-to-all-start = ((bf16[8,16,512]{2,1,0:T(8,128)(2,1)}), bf16[8,16,512]{2,1,0:T(8,128)(2,1)S(1)}, u32[]{:S(2)}, u32[]{:S(2)}) async-start(bf16[8,16,512]{2,1,0:T(8,128)(2,1)} %broadcast_in_dim.21), calls=%async_computation | async-start | bytes 262144 | tf_op jit(solution)/shard_map/all_to_all | solution.py:250
  11.1 0.9 %slice_bitcast_fusion = bf16[128,512]{1,0:T(8,128)(2,1)S(1)} fusion(bf16[1,256,512]{2,1,0:T(8,128)(2,1)} %param.8), kind=kLoop, calls=%fused_computation.1 | loop fusion | bytes 262144 | tf_op jit(solution)/shard_map/slice | solution.py:242
  12.1 1.0 %collective-permute-start = (bf16[128,512]{1,0:T(8,128)(2,1)S(1)}, bf16[128,512]{1,0:T(8,128)(2,1)S(1)}, u32[]{:S(2)}, u32[]{:S(2)}) collective-permute-start(bf16[128,512]{1,0:T(8,128)(2,1)S(1)} %slice_bitcast_fusion), channel_id=1, source_target_pairs={{0,1},{1,0},{2,3},{3,2},{4,5},{5,4},{6,7},{7,6},{8,9},{9,8},{10,11... | collective-permute-start | bytes 393224 | tf_op jit(solution)/shard_map/ppermute | solution.py:242
  13.1 5.8 %all-to-all-done = bf16[8,16,512]{2,1,0:T(8,128)(2,1)S(1)} async-done(((bf16[8,16,512]{2,1,0:T(8,128)(2,1)}), bf16[8,16,512]{2,1,0:T(8,128)(2,1)S(1)}, u32[]{:S(2)}, u32[]{:S(2)}) %all-to-all-start) | async-done | bytes 131104 | tf_op jit(solution)/shard_map/all_to_all | solution.py:250
  18.9 1.3 %collective-permute-start.1 = (bf16[128,512]{1,0:T(8,128)(2,1)S(1)}, bf16[128,512]{1,0:T(8,128)(2,1)S(1)}, u32[]{:S(2)}, u32[]{:S(2)}) collective-permute-start(bf16[128,512]{1,0:T(8,128)(2,1)S(1)} %bitcast.16), channel_id=1, source_target_pairs={{0,2},{1,9},{2,4},{3,11},{4,6},{5,13},{6,0},{7,15},{8,10},{9,17},{... | collective-permute-start | bytes 393224 | tf_op jit(solution)/shard_map/ppermute | solution.py:46
  20.2 1.4 %collective-permute-start.2 = (bf16[128,512]{1,0:T(8,128)(2,1)S(1)}, bf16[128,512]{1,0:T(8,128)(2,1)S(1)}, u32[]{:S(2)}, u32[]{:S(2)}) collective-permute-start(bf16[128,512]{1,0:T(8,128)(2,1)S(1)} %bitcast.17), channel_id=1, source_target_pairs={{0,6},{1,25},{2,0},{3,27},{4,2},{5,29},{6,4},{7,31},{8,14},{9,1},{... | collective-permute-start | bytes 393224 | tf_op jit(solution)/shard_map/ppermute | solution.py:46
  21.7 1.6 %collective-permute-start.3 = (bf16[128,512]{1,0:T(8,128)(2,1)S(1)}, bf16[128,512]{1,0:T(8,128)(2,1)S(1)}, u32[]{:S(2)}, u32[]{:S(2)}) collective-permute-start(bf16[128,512]{1,0:T(8,128)(2,1)S(1)} %bitcast.18), channel_id=1, source_target_pairs={{0,4},{1,17},{2,6},{3,19},{4,0},{5,21},{6,2},{7,23},{8,12},{9,25},... | collective-permute-start | bytes 393224 | tf_op jit(solution)/shard_map/ppermute | solution.py:46
  23.3 0.8 %select_subtract_fusion.3 = (s32[4,4]{1,0:T(4,128)S(1)}, s32[4,4]{1,0:T(4,128)S(1)}, s32[4,4]{1,0:T(4,128)S(1)}, s32[4,4]{1,0:T(4,128)S(1)}) fusion(s32[4]{0:T(128)} %constant.60.clone, s32[]{:T(128)S(6)} %axis_index.46, pred[]{:T(512)S(6)} %eq.13, pred[]{:T(512)S(6)} %eq.14, s32[]{:T(128)S(6)} %axis_index.51), kind=kLoop, calls=%fused_computation.16 | loop fusion | flops 128 | bytes 282 | tf_op jit(solution)/shard_map/sub | solution.py:232
  24.1 0.1 sub.40
  24.2 0.1 sub.43
  24.3 0.1 sub.46
  24.4 0.1 sub.48
  24.4 0.0 collective-permute-done.1
  24.4 0.0 collective-permute-done.2
  24.4 2.5 %collective-permute-done.3 = bf16[128,512]{1,0:T(8,128)(2,1)S(1)} collective-permute-done((bf16[128,512]{1,0:T(8,128)(2,1)S(1)}, bf16[128,512]{1,0:T(8,128)(2,1)S(1)}, u32[]{:S(2)}, u32[]{:S(2)}) %collective-permute-start.3) | collective-permute-done | bytes 131104 | tf_op jit(solution)/shard_map/ppermute | solution.py:46
  27.0 4.0 %collective-permute-start.4 = (bf16[512,512]{1,0:T(8,128)(2,1)S(1)}, bf16[512,512]{1,0:T(8,128)(2,1)S(1)}, u32[]{:S(2)}, u32[]{:S(2)}) collective-permute-start(bf16[512,512]{1,0:T(8,128)(2,1)S(1)} %pad_maximum_fusion.rest_0_.rest_4_), channel_id=1, source_target_pairs={{0,1},{1,0},{2,3},{3,2},{4,5},{5,4},{6,7},{7,6},{8,9},{9,8},{10,11... | collective-permute-start | bytes 1572872 | tf_op jit(solution)/shard_map/ppermute | solution.py:50
  31.0 0.0 collective-permute-start.5
  31.0 2.7 %collective-permute-start.7 = (bf16[512,512]{1,0:T(8,128)(2,1)S(1)}, bf16[512,512]{1,0:T(8,128)(2,1)S(1)}, u32[]{:S(2)}, u32[]{:S(2)}) collective-permute-start(bf16[512,512]{1,0:T(8,128)(2,1)S(1)} %pad_maximum_fusion.rest_0_.rest_4_), channel_id=1, source_target_pairs={{0,24},{1,7},{2,26},{3,1},{4,28},{5,3},{6,30},{7,5},{8,0},{9,15},{... | collective-permute-start | bytes 1572872 | tf_op jit(solution)/shard_map/ppermute | solution.py:46
  34.4 0.1 pad_add_fusion.scalars
  34.5 0.0 collective-permute-done.rim_ref
  34.5 0.0 copy-start
  34.5 1.0 %copy-done = bf16[1,256,512]{2,1,0:T(8,128)(2,1)S(1)} copy-done((bf16[1,256,512]{2,1,0:T(8,128)(2,1)S(1)}, bf16[1,256,512]{2,1,0:T(8,128)(2,1)}, u32[]{:S(2)}) %copy-start) | copy-done | bytes 262168
  35.4 0.0 copy-start.1
  35.4 1.2 %copy-done.1 = bf16[1,256,1792]{2,1,0:T(8,128)(2,1)S(1)} copy-done((bf16[1,256,1792]{2,1,0:T(8,128)(2,1)S(1)}, bf16[1,256,1792]{2,1,0:T(8,128)(2,1)}, u32[]{:S(2)}) %copy-start.1) | copy-done | bytes 917528
  36.6 2.2 %local.1 = (bf16[2,1792,256]{2,1,0:T(8,128)(2,1)S(1)}, f32[2,1792,256]{2,1,0:T(8,128)S(1)}) custom-call(s32[34]{0:T(128)S(1)} %pad_add_fusion.scalars, bf16[256,1792]{1,0:T(8,128)(2,1)S(1)} %bitcast.15, bf16[128,512]{1,0:T(8,128)(2,1)S(1)} %collective-permute-done.rim_ref, bf16[256,512]{1,0:T(8,128)(2,1)S(1)} %bitcast.14), custom_call_target="tpu_custom_call" | custom-call | flops 3758096384 | bytes 1048576 | tf_op jit(solution)/shard_map/local/pallas_call | solution.py:188
  38.8 1.8 %collective-permute-done.5.rest_0_.rest_6_ = bf16[512,512]{1,0:T(8,128)(2,1)S(1)} collective-permute-done((bf16[512,512]{1,0:T(8,128)(2,1)S(1)}, bf16[512,512]{1,0:T(8,128)(2,1)S(1)}, u32[]{:S(2)}, u32[]{:S(2)}) %collective-permute-start.5) | collective-permute-done | bytes 524320 | tf_op jit(solution)/shard_map/ppermute | solution.py:46
  40.6 0.1 collective-permute-start.9
  40.7 0.0 collective-permute-done.7.rest_2_.rest_8_
  40.7 2.7 %collective-permute-start.11 = (bf16[256,512]{1,0:T(8,128)(2,1)S(1)}, bf16[256,512]{1,0:T(8,128)(2,1)S(1)}, u32[]{:S(2)}, u32[]{:S(2)}) collective-permute-start(bf16[256,512]{1,0:T(8,128)(2,1)S(1)} %slice.17), channel_id=1, source_target_pairs={{0,24},{1,7},{2,26},{3,1},{4,28},{5,3},{6,30},{7,5},{8,0},{9,15},{... | collective-permute-start | bytes 786440 | tf_op jit(solution)/shard_map/ppermute | solution.py:46
  43.5 1.5 %collective-permute-start.6 = (bf16[512,512]{1,0:T(8,128)(2,1)S(1)}, bf16[512,512]{1,0:T(8,128)(2,1)S(1)}, u32[]{:S(2)}, u32[]{:S(2)}) collective-permute-start(bf16[512,512]{1,0:T(8,128)(2,1)S(1)} %collective-permute-done.5.rest_0_.rest_6_), channel_id=1, source_target_pairs={{0,1},{1,0},{2,3},{3,2},{4,5},{5,4},{6,7},{7,6},{8,9},{9,8},{10,11... | collective-permute-start | bytes 1572872 | tf_op jit(solution)/shard_map/ppermute | solution.py:50
  45.0 0.0 collective-permute-start.8
  45.0 0.0 collective-permute-done.4.rest_1_.rest_5_
  45.0 5.9 %remote.2.acc_ref = f32[2,1792,256]{2,1,0:T(8,128)S(1)} custom-call(s32[34]{0:T(128)S(1)} %pad_add_fusion.scalars, bf16[2,1792,256]{2,1,0:T(8,128)(2,1)S(1)} %get-tuple-element.7.qa_ref, f32[2,1792,256]{2,1,0:T(8,128)S(1)} %get-tuple-element.8.acc_ref.local_ref, bf16[512,512]{1,0:T(8,128)(2,1)S(1)} %pad_maximum_fusion.rest_0_.rest_4_, ...), custom_call_target="tpu_custom_call" | custom-call | flops 7516192768 | bytes 1048576 | tf_op jit(solution)/shard_map/remote/pallas_call | solution.py:201
  50.8 0.0 collective-permute-done.9.rest_0_
  50.8 0.8 %collective-permute-start.10 = (bf16[256,512]{1,0:T(8,128)(2,1)S(1)}, bf16[256,512]{1,0:T(8,128)(2,1)S(1)}, u32[]{:S(2)}, u32[]{:S(2)}) collective-permute-start(bf16[256,512]{1,0:T(8,128)(2,1)S(1)} %collective-permute-done.9.rest_0_), channel_id=1, source_target_pairs={{0,1},{1,0},{2,3},{3,2},{4,5},{5,4},{6,7},{7,6},{8,9},{9,8},{10,11... | collective-permute-start | bytes 786440 | tf_op jit(solution)/shard_map/ppermute | solution.py:50
  51.6 0.0 collective-permute-done.11.rest_2_
  51.6 0.1 collective-permute-start.12
  51.7 0.0 collective-permute-done.6.rest_1_.rest_7_
  51.7 0.0 collective-permute-done.8.rest_3_.rest_9_
  51.7 9.9 %remote.3.acc_ref = f32[2,1792,256]{2,1,0:T(8,128)S(1)} custom-call(s32[34]{0:T(128)S(1)} %pad_add_fusion.scalars, bf16[2,1792,256]{2,1,0:T(8,128)(2,1)S(1)} %get-tuple-element.7.qa_ref, f32[2,1792,256]{2,1,0:T(8,128)S(1)} %remote.2.acc_ref, bf16[512,512]{1,0:T(8,128)(2,1)S(1)} %collective-permute-done.5.rest_0_.rest_6_, ...), custom_call_target="tpu_custom_call" | custom-call | flops 15032385536 | bytes 1048576 | tf_op jit(solution)/shard_map/remote/pallas_call | solution.py:201
  61.7 0.0 collective-permute-done.10.rest_1_
  61.7 0.0 collective-permute-done.12.rest_3_
  61.7 8.4 %last.1 = bf16[256,1792]{1,0:T(8,128)(2,1)} custom-call(s32[34]{0:T(128)S(1)} %pad_add_fusion.scalars, bf16[2,1792,256]{2,1,0:T(8,128)(2,1)S(1)} %get-tuple-element.7.qa_ref, f32[2,1792,256]{2,1,0:T(8,128)S(1)} %get-tuple-element.8.acc_ref.local_ref, f32[2,1792,256]{2,1,0:T(8,128)S(1)} %remote.3.acc_ref, ...), custom_call_target="tpu_custom_call" | custom-call | flops 30064771072 | bytes 1048576 | tf_op jit(solution)/shard_map/last/pallas_call | solution.py:215
  (6 shorter events, 0.1 us)
Async XLA Ops:
  2.1 16.8 %all-to-all-start = ((bf16[8,16,512]{2,1,0:T(8,128)(2,1)}), bf16[8,16,512]{2,1,0:T(8,128)(2,1)S(1)}, u32[]{:S(2)}, u32[]{:S(2)}) async-start(bf16[8,16,512]{2,1,0:T(8,128)(2,1)} %broadcast_in_dim.21), calls=%async_computation | async-start | bytes 262144 | tf_op jit(solution)/shard_map/all_to_all | solution.py:250
  12.1 22.4 %collective-permute-start = (bf16[128,512]{1,0:T(8,128)(2,1)S(1)}, bf16[128,512]{1,0:T(8,128)(2,1)S(1)}, u32[]{:S(2)}, u32[]{:S(2)}) collective-permute-start(bf16[128,512]{1,0:T(8,128)(2,1)S(1)} %slice_bitcast_fusion), channel_id=1, source_target_pairs={{0,1},{1,0},{2,3},{3,2},{4,5},{5,4},{6,7},{7,6},{8,9},{9,8},{10,11... | collective-permute-start | bytes 393224 | tf_op jit(solution)/shard_map/ppermute | solution.py:242
  18.9 5.5 %collective-permute-start.1 = (bf16[128,512]{1,0:T(8,128)(2,1)S(1)}, bf16[128,512]{1,0:T(8,128)(2,1)S(1)}, u32[]{:S(2)}, u32[]{:S(2)}) collective-permute-start(bf16[128,512]{1,0:T(8,128)(2,1)S(1)} %bitcast.16), channel_id=1, source_target_pairs={{0,2},{1,9},{2,4},{3,11},{4,6},{5,13},{6,0},{7,15},{8,10},{9,17},{... | collective-permute-start | bytes 393224 | tf_op jit(solution)/shard_map/ppermute | solution.py:46
  20.2 4.2 %collective-permute-start.2 = (bf16[128,512]{1,0:T(8,128)(2,1)S(1)}, bf16[128,512]{1,0:T(8,128)(2,1)S(1)}, u32[]{:S(2)}, u32[]{:S(2)}) collective-permute-start(bf16[128,512]{1,0:T(8,128)(2,1)S(1)} %bitcast.17), channel_id=1, source_target_pairs={{0,6},{1,25},{2,0},{3,27},{4,2},{5,29},{6,4},{7,31},{8,14},{9,1},{... | collective-permute-start | bytes 393224 | tf_op jit(solution)/shard_map/ppermute | solution.py:46
  21.7 5.3 %collective-permute-start.3 = (bf16[128,512]{1,0:T(8,128)(2,1)S(1)}, bf16[128,512]{1,0:T(8,128)(2,1)S(1)}, u32[]{:S(2)}, u32[]{:S(2)}) collective-permute-start(bf16[128,512]{1,0:T(8,128)(2,1)S(1)} %bitcast.18), channel_id=1, source_target_pairs={{0,4},{1,17},{2,6},{3,19},{4,0},{5,21},{6,2},{7,23},{8,12},{9,25},... | collective-permute-start | bytes 393224 | tf_op jit(solution)/shard_map/ppermute | solution.py:46
  27.0 17.9 %collective-permute-start.4 = (bf16[512,512]{1,0:T(8,128)(2,1)S(1)}, bf16[512,512]{1,0:T(8,128)(2,1)S(1)}, u32[]{:S(2)}, u32[]{:S(2)}) collective-permute-start(bf16[512,512]{1,0:T(8,128)(2,1)S(1)} %pad_maximum_fusion.rest_0_.rest_4_), channel_id=1, source_target_pairs={{0,1},{1,0},{2,3},{3,2},{4,5},{5,4},{6,7},{7,6},{8,9},{9,8},{10,11... | collective-permute-start | bytes 1572872 | tf_op jit(solution)/shard_map/ppermute | solution.py:50
  31.0 9.5 %collective-permute-start.5 = (bf16[512,512]{1,0:T(8,128)(2,1)S(1)}, bf16[512,512]{1,0:T(8,128)(2,1)S(1)}, u32[]{:S(2)}, u32[]{:S(2)}) collective-permute-start(bf16[512,512]{1,0:T(8,128)(2,1)S(1)} %pad_maximum_fusion.rest_0_.rest_4_), channel_id=1, source_target_pairs={{0,8},{1,3},{2,10},{3,5},{4,12},{5,7},{6,14},{7,1},{8,16},{9,11},{... | collective-permute-start | bytes 1572872 | tf_op jit(solution)/shard_map/ppermute | solution.py:46
  31.0 9.6 %collective-permute-start.7 = (bf16[512,512]{1,0:T(8,128)(2,1)S(1)}, bf16[512,512]{1,0:T(8,128)(2,1)S(1)}, u32[]{:S(2)}, u32[]{:S(2)}) collective-permute-start(bf16[512,512]{1,0:T(8,128)(2,1)S(1)} %pad_maximum_fusion.rest_0_.rest_4_), channel_id=1, source_target_pairs={{0,24},{1,7},{2,26},{3,1},{4,28},{5,3},{6,30},{7,5},{8,0},{9,15},{... | collective-permute-start | bytes 1572872 | tf_op jit(solution)/shard_map/ppermute | solution.py:46
  34.5 1.0 %copy-start = (bf16[1,256,512]{2,1,0:T(8,128)(2,1)S(1)}, bf16[1,256,512]{2,1,0:T(8,128)(2,1)}, u32[]{:S(2)}) copy-start(bf16[1,256,512]{2,1,0:T(8,128)(2,1)} %param.8) | copy-start | bytes 786436
  35.4 1.2 %copy-start.1 = (bf16[1,256,1792]{2,1,0:T(8,128)(2,1)S(1)}, bf16[1,256,1792]{2,1,0:T(8,128)(2,1)}, u32[]{:S(2)}) copy-start(bf16[1,256,1792]{2,1,0:T(8,128)(2,1)} %param.7) | copy-start | bytes 2752516
  40.6 10.2 %collective-permute-start.9 = (bf16[256,512]{1,0:T(8,128)(2,1)S(1)}, bf16[256,512]{1,0:T(8,128)(2,1)S(1)}, u32[]{:S(2)}, u32[]{:S(2)}) collective-permute-start(bf16[256,512]{1,0:T(8,128)(2,1)S(1)} %slice.16), channel_id=1, source_target_pairs={{0,8},{1,3},{2,10},{3,5},{4,12},{5,7},{6,14},{7,1},{8,16},{9,11},{... | collective-permute-start | bytes 786440 | tf_op jit(solution)/shard_map/ppermute | solution.py:46
  40.7 10.9 %collective-permute-start.11 = (bf16[256,512]{1,0:T(8,128)(2,1)S(1)}, bf16[256,512]{1,0:T(8,128)(2,1)S(1)}, u32[]{:S(2)}, u32[]{:S(2)}) collective-permute-start(bf16[256,512]{1,0:T(8,128)(2,1)S(1)} %slice.17), channel_id=1, source_target_pairs={{0,24},{1,7},{2,26},{3,1},{4,28},{5,3},{6,30},{7,5},{8,0},{9,15},{... | collective-permute-start | bytes 786440 | tf_op jit(solution)/shard_map/ppermute | solution.py:46
  43.5 8.3 %collective-permute-start.6 = (bf16[512,512]{1,0:T(8,128)(2,1)S(1)}, bf16[512,512]{1,0:T(8,128)(2,1)S(1)}, u32[]{:S(2)}, u32[]{:S(2)}) collective-permute-start(bf16[512,512]{1,0:T(8,128)(2,1)S(1)} %collective-permute-done.5.rest_0_.rest_6_), channel_id=1, source_target_pairs={{0,1},{1,0},{2,3},{3,2},{4,5},{5,4},{6,7},{7,6},{8,9},{9,8},{10,11... | collective-permute-start | bytes 1572872 | tf_op jit(solution)/shard_map/ppermute | solution.py:50
  45.0 6.8 %collective-permute-start.8 = (bf16[512,512]{1,0:T(8,128)(2,1)S(1)}, bf16[512,512]{1,0:T(8,128)(2,1)S(1)}, u32[]{:S(2)}, u32[]{:S(2)}) collective-permute-start(bf16[512,512]{1,0:T(8,128)(2,1)S(1)} %collective-permute-done.7.rest_2_.rest_8_), channel_id=1, source_target_pairs={{0,1},{1,0},{2,3},{3,2},{4,5},{5,4},{6,7},{7,6},{8,9},{9,8},{10,11... | collective-permute-start | bytes 1572872 | tf_op jit(solution)/shard_map/ppermute | solution.py:50
  50.8 10.8 %collective-permute-start.10 = (bf16[256,512]{1,0:T(8,128)(2,1)S(1)}, bf16[256,512]{1,0:T(8,128)(2,1)S(1)}, u32[]{:S(2)}, u32[]{:S(2)}) collective-permute-start(bf16[256,512]{1,0:T(8,128)(2,1)S(1)} %collective-permute-done.9.rest_0_), channel_id=1, source_target_pairs={{0,1},{1,0},{2,3},{3,2},{4,5},{5,4},{6,7},{7,6},{8,9},{9,8},{10,11... | collective-permute-start | bytes 786440 | tf_op jit(solution)/shard_map/ppermute | solution.py:50
  51.6 10.1 %collective-permute-start.12 = (bf16[256,512]{1,0:T(8,128)(2,1)S(1)}, bf16[256,512]{1,0:T(8,128)(2,1)S(1)}, u32[]{:S(2)}, u32[]{:S(2)}) collective-permute-start(bf16[256,512]{1,0:T(8,128)(2,1)S(1)} %collective-permute-done.11.rest_2_), channel_id=1, source_target_pairs={{0,1},{1,0},{2,3},{3,2},{4,5},{5,4},{6,7},{7,6},{8,9},{9,8},{10,11... | collective-permute-start | bytes 786440 | tf_op jit(solution)/shard_map/ppermute | solution.py:50

commit v2 on v1

v2 whole, which is shorter than its diff:
```python
import functools
import math

import jax
import jax.numpy as jnp
from jax import lax
from jax.experimental import pallas as pl
from jax.experimental.pallas import tpu as pltpu
from jax.sharding import Mesh
from jax.sharding import PartitionSpec as P

KVH = 2
HD = 128
GROUP = 7
WINDOW = 128
CLIP = ("z", "y", "x")
PLANE = ("y", "x", "row")
ZS, YS, XS = 8, 4, 4
TOKENS = 256
HALF = 16
COLUMN = ZS * HALF
RATE = HD**-0.5 * math.log2(math.e)
MARGIN = 250.0
DEAD = 64.0
ALIVE_BELOW = 32.0
CLOSED = -1e30
LARGE = 1e30
DA = (0, 1, 3, 2)
VMEM = pl.BlockSpec(memory_space=pltpu.VMEM)
SMEM = pl.BlockSpec(memory_space=pltpu.SMEM)
NT = (((1,), (1,)), ((), ()))
BQ = 896
BK = 256


def plane_shift(block, phase, distance):
    route = []
    for y in range(YS):
        for x in range(XS):
            for row in range(2):
                if (row == 0) == (phase == 0):
                    to = (y, (x + distance) % XS)
                else:
                    to = ((y + distance) % YS, x)
                route.append(((y * XS + x) * 2 + row, (to[0] * XS + to[1]) * 2 + row))
    return lax.ppermute(block, PLANE, route)


def other_core(block):
    return lax.ppermute(block, "row", [(0, 1), (1, 0)])


def band_masks(ids):
    t = lax.broadcasted_iota(jnp.int32, (WINDOW, 2 * WINDOW), 0)
    j = lax.broadcasted_iota(jnp.int32, (WINDOW, 2 * WINDOW), 1)
    band = (j > t) & (j <= t + WINDOW)
    return (band & (j >= jnp.where(ids[0] == 0, WINDOW, 0)), band)


def band_frames(rim_ref, own_ref, columns):
    own = own_ref[:, columns]
    return (jnp.concatenate([rim_ref[:, columns], own[:WINDOW]], axis=0), own)


def local_kernel(ids, q_hbm, rim_ref, own_ref, qa_ref, acc_ref, q_ref, sems):
    wide = GROUP * HD
    copies = [
        pltpu.make_async_copy(q_hbm.at[:, pl.ds(h * wide, wide)], q_ref.at[h], sems.at[h]) for h in range(KVH)
    ]
    for copy in copies:
        copy.start()
    masks = band_masks(ids)
    lane = lax.broadcasted_iota(jnp.int32, (WINDOW, HD), 1)
    ones = jnp.ones((2 * WINDOW, HD), jnp.bfloat16)
    for h in range(KVH):
        keys = band_frames(rim_ref, own_ref, slice(h * HD, (h + 1) * HD))
        values = band_frames(rim_ref, own_ref, slice((KVH + h) * HD, (KVH + h + 1) * HD))
        copies[h].wait()
        for g in range(GROUP):
            for part in range(2):
                q = q_ref[h, part * WINDOW : (part + 1) * WINDOW, g * HD : (g + 1) * HD]
                s = lax.dot_general(q, keys[part], NT, preferred_element_type=jnp.float32)
                top = jnp.max(jnp.where(masks[part], s, CLOSED), axis=1, keepdims=True)
                ref = (top + MARGIN).astype(jnp.bfloat16).astype(jnp.float32)
                p = jnp.where(masks[part], jnp.exp2((s - ref) * RATE), 0.0).astype(jnp.bfloat16)
                value = jnp.concatenate([values[part], ones], axis=1)
                rows = slice(g * TOKENS + part * WINDOW, g * TOKENS + (part + 1) * WINDOW)
                acc_ref[h, rows, :] = jnp.dot(p, value, preferred_element_type=jnp.float32)
                extra = jnp.where(lane == 0, ref, jnp.where(lane == 1, 1.0, 0.0))
                qa_ref[h, rows, :HD] = q
                qa_ref[h, rows, HD:] = extra.astype(jnp.bfloat16)


def plane_limit(ids, role, db, da):
    row, z, y, x = ids[0], ids[1], ids[2], ids[3]
    straight = (row + role) % 2 == 0
    from_y = (y - jnp.where(straight, db, da) + YS) % YS
    from_x = (x - jnp.where(straight, da, db) + XS) % XS
    return z + jnp.where(from_y * XS + from_x < y * XS + x, 1, 0)


def build_extra(ids, chunks, extra):
    row = lax.broadcasted_iota(jnp.int32, (BK, HD), 0)
    lane = lax.broadcasted_iota(jnp.int32, (BK, HD), 1)
    plane = row // (HALF * len(DA))
    block = (row // HALF) % len(DA)
    at = 0
    for ref, role, db, base in chunks:
        limit = plane_limit(ids, role, db, DA[3])
        for d in range(3):
            limit = jnp.where(block == d, plane_limit(ids, role, db, DA[d]), limit)
        for b in range(ref.shape[0] // BK):
            flag = ref[b * BK : (b + 1) * BK, KVH * HD : KVH * HD + HD].astype(jnp.float32)
            valid = (plane + (base + b) * (ZS // 2) < limit) & (flag < ALIVE_BELOW)
            bias = jnp.where(valid, 0.0, CLOSED)
            tile = jnp.where(lane == 0, -1.0, jnp.where(lane == 1, bias, 0.0))
            extra[at : at + BK, :] = tile.astype(jnp.bfloat16)
            at += BK


def key_tiles(chunks, upper):
    at = 0
    found = []
    for ref, _, _, base in chunks:
        for b in range(ref.shape[0] // BK):
            if upper or base + b == 0:
                found.append((ref, b * BK, at))
            at += BK
    return found


def head_columns(j):
    return pl.ds(pl.multiple_of(j * HD, HD), HD)


def scores(q, ref, start, at, h, extra):
    key = jnp.concatenate([ref[start : start + BK, head_columns(h)], extra[at : at + BK, :]], axis=1)
    return lax.dot_general(q, key, NT, preferred_element_type=jnp.float32)


def weighted(p, ref, start, h):
    ones = jnp.ones((BK, HD), jnp.bfloat16)
    value = jnp.concatenate([ref[start : start + BK, head_columns(KVH + h)], ones], axis=1)
    return jnp.dot(p.astype(jnp.bfloat16), value, preferred_element_type=jnp.float32)


def accumulate(acc, q, tiles, h, extra):
    for ref, start, at in tiles:
        p = jnp.exp2(scores(q, ref, start, at, h, extra) * RATE)
        acc = acc + weighted(p, ref, start, h)
    return acc


def by_height(ids, run):
    high = ids[1] >= ZS // 2
    pl.when(high)(lambda: run(True))
    pl.when(jnp.logical_not(high))(lambda: run(False))


def each_block(body):
    blocks = ROWS // BQ

    def step(n, carry):
        body(n // blocks, lax.rem(n, blocks))
        return carry

    lax.fori_loop(0, KVH * blocks, step, 0)


def remote_kernel(places, ids, qa_ref, acc_ref, *rest):
    refs, (out_ref, extra) = rest[: len(places)], rest[len(places) :]
    chunks = [(ref, *place) for ref, place in zip(refs, places)]
    build_extra(ids, chunks, extra)

    def run(upper):
        tiles = key_tiles(chunks, upper)

        def body(h, i):
            rows = pl.ds(i * BQ, BQ)
            out_ref[h, rows, :] = accumulate(acc_ref[h, rows, :], qa_ref[h, rows, :], tiles, h, extra)

        each_block(body)

    by_height(ids, run)


def last_kernel(places, new, ids, lengths, qa_ref, rim_ref, own_ref, acc_ref, *rest):
    refs, (out_ref, extra, worst) = rest[: len(places)], rest[len(places) :]
    chunks = [(ref, *place) for ref, place in zip(refs, places)]
    build_extra(ids, chunks[:new], extra)
    count = lengths[0] - ids[0] * TOKENS
    token = lax.broadcasted_iota(jnp.int32, (WINDOW, HD), 0)
    worst[...] = jnp.zeros_like(worst)

    def finish(h, piece, acc):
        result = acc[:, :HD] / acc[:, HD:]
        first = lax.rem(piece, 2) * WINDOW
        column = (h * GROUP + piece // 2) * HD
        present = token + first < count
        where = (pl.ds(pl.multiple_of(first, WINDOW), WINDOW), pl.ds(pl.multiple_of(column, HD), HD))
        out_ref[where] = jnp.where(present, result, 0.0).astype(jnp.bfloat16)

    def run(upper):
        tiles = key_tiles(chunks[:new], upper)

        def body(h, i):
            rows = pl.ds(i * BQ, BQ)
            acc = accumulate(acc_ref[h, rows, :], qa_ref[h, rows, :], tiles, h, extra)
            largest = worst[...]
            for k in range(BQ // WINDOW):
                piece = acc[k * WINDOW : (k + 1) * WINDOW]
                finish(h, i * (BQ // WINDOW) + k, piece)
                largest = largest + piece[:, HD:]
            worst[...] = largest

        each_block(body)

    by_height(ids, run)

    @pl.when(jnp.logical_not(jnp.max(worst[...]) < LARGE))
    def _():
        build_extra(ids, chunks, extra)
        tiles = key_tiles(chunks, True)
        masks = band_masks(ids)

        def redo(n, carry):
            h, piece = n // (2 * GROUP), lax.rem(n, 2 * GROUP)
            rows = pl.ds(piece * WINDOW, WINDOW)
            q = qa_ref[h, rows, :]
            top = jnp.zeros((WINDOW, 1), jnp.float32)
            for ref, start, at in tiles:
                s = scores(q, ref, start, at, h, extra)
                top = jnp.maximum(top, jnp.max(s, axis=1, keepdims=True))
            first = lax.rem(piece, 2) == 0
            keys = band_frames(rim_ref, own_ref, head_columns(h))
            values = band_frames(rim_ref, own_ref, head_columns(KVH + h))
            key = jnp.where(first, keys[0], keys[1])
            value = jnp.concatenate([jnp.where(first, values[0], values[1]), jnp.ones((BK, HD), jnp.bfloat16)], axis=1)
            mask = jnp.where(first, masks[0].astype(jnp.int32), masks[1].astype(jnp.int32)) > 0
            s = lax.dot_general(q[:, :HD], key, NT, preferred_element_type=jnp.float32)
            shift = q[:, HD : HD + 1].astype(jnp.float32) + top
            p = jnp.where(mask, jnp.exp2((s - shift) * RATE), 0.0)
            acc = jnp.dot(p.astype(jnp.bfloat16), value, preferred_element_type=jnp.float32)
            for ref, start, at in tiles:
                p = jnp.exp2((scores(q, ref, start, at, h, extra) - top) * RATE)
                acc = acc + weighted(p, ref, start, h)
            finish(h, piece, acc)
            return carry

        lax.fori_loop(0, KVH * 2 * GROUP, redo, 0)


def cost(keys):
    rows = KVH * GROUP * TOKENS
    return pl.CostEstimate(flops=8 * rows * keys * 2 * HD, bytes_accessed=1 << 20, transcendentals=rows * keys)


PARAMS = pltpu.CompilerParams(vmem_limit_bytes=16 * 2**20)
ROWS = GROUP * TOKENS
ACC = jax.ShapeDtypeStruct((KVH, ROWS, 2 * HD), jnp.float32)


def attend_local(ids, q, rim, own):
    return pl.pallas_call(
        local_kernel,
        out_shape=(jax.ShapeDtypeStruct((KVH, ROWS, 2 * HD), jnp.bfloat16), ACC),
        in_specs=[SMEM, pl.BlockSpec(memory_space=pltpu.HBM), VMEM, VMEM],
        out_specs=(VMEM, VMEM),
        scratch_shapes=[pltpu.VMEM((KVH, TOKENS, GROUP * HD), jnp.bfloat16), pltpu.SemaphoreType.DMA((KVH,))],
        compiler_params=PARAMS,
        cost_estimate=cost(512),
        name="local",
    )(ids, q, rim, own)


def attend_remote(ids, qa, acc, chunks, places):
    keys = sum(c.shape[0] for c in chunks)
    return pl.pallas_call(
        functools.partial(remote_kernel, places),
        out_shape=ACC,
        in_specs=[SMEM] + [VMEM] * (2 + len(chunks)),
        out_specs=VMEM,
        scratch_shapes=[pltpu.VMEM((keys, HD), jnp.bfloat16)],
        compiler_params=PARAMS,
        cost_estimate=cost(keys),
        name="remote",
    )(ids, qa, acc, *chunks)


def attend_last(ids, lengths, qa, rim, own, acc, chunks, places, new):
    keys = sum(c.shape[0] for c in chunks)
    return pl.pallas_call(
        functools.partial(last_kernel, places, new),
        out_shape=jax.ShapeDtypeStruct((TOKENS, KVH * GROUP * HD), jnp.bfloat16),
        in_specs=[SMEM] * 2 + [VMEM] * (4 + len(chunks)),
        out_specs=VMEM,
        scratch_shapes=[pltpu.VMEM((keys, HD), jnp.bfloat16), pltpu.VMEM((WINDOW, HD), jnp.float32)],
        compiler_params=PARAMS,
        cost_estimate=cost(keys),
        name="last",
    )(ids, lengths, qa, rim, own, acc, *chunks)


def shards(queries, frames_kv, summary_kv, lengths, caps):
    row = lax.axis_index("row")
    ids = jnp.stack([row, lax.axis_index("z"), lax.axis_index("y"), lax.axis_index("x")]).astype(jnp.int32)
    slot = lax.broadcasted_iota(jnp.int32, (ZS, HALF, 4 * HD), 1) + HALF * row
    entry = lax.broadcasted_iota(jnp.int32, (ZS, HALF, 4 * HD), 2)
    mine = jnp.broadcast_to(summary_kv, (ZS, HALF, 4 * HD))
    copies = jnp.where((slot >= caps[0]) & (entry >= KVH * HD), jnp.bfloat16(DEAD), mine)
    own, copies = lax.optimization_barrier((frames_kv[0], copies))
    column = lax.all_to_all(copies, "z", 0, 0, tiled=True)
    rim = lax.ppermute(own[TOKENS - WINDOW :], "row", [(0, 1), (1, 0)])

    own, column = lax.optimization_barrier((own, column))
    columns = [column] + [plane_shift(column, 0, d) for d in DA[1:]]
    qa, acc = attend_local(ids, queries[0], rim, own)
    columns, qa, acc = lax.optimization_barrier((columns, qa, acc))
    near = jnp.stack(columns, axis=1)
    near = near.reshape(len(DA) * COLUMN, 4 * HD)
    half = near.shape[0] // 2
    near_other = other_core(near)
    one = plane_shift(near, 1, 1)
    three = plane_shift(near, 1, 3)
    zero_places = ((0, 0, 0), (1, 0, 0))
    acc = attend_remote(ids, qa, acc, (near, near_other), zero_places)
    one, three, acc = lax.optimization_barrier((one, three, acc))
    two_low = plane_shift(one[:half], 1, 1)
    two_high = plane_shift(three[half:], 1, 3)
    one_other, three_other = other_core(one), other_core(three)
    one_places, three_places = ((0, 1, 0), (1, 1, 0)), ((0, 3, 0), (1, 3, 0))
    acc = attend_remote(ids, qa, acc, (one, one_other), one_places)
    two_low, two_high, acc = lax.optimization_barrier((two_low, two_high, acc))
    low_other, high_other = other_core(two_low), other_core(two_high)
    acc = attend_remote(ids, qa, acc, (three, three_other), three_places)

    chunks = (two_low, low_other, two_high, high_other)
    chunks += (near, near_other, one, one_other, three, three_other)
    places = ((0, 2, 0), (1, 2, 0), (0, 2, 1), (1, 2, 1)) + zero_places + one_places + three_places
    return attend_last(ids, lengths, qa, rim, own, acc, chunks, places, 4)[None]


def solution(mesh):
    torus = Mesh(mesh.devices.reshape(ZS, YS, XS, 2), CLIP + ("row",))
    placed = (P(CLIP, "row", None), P(CLIP, "row", None), P(CLIP, "row", None), P(CLIP), P(CLIP))
    return jax.shard_map(
        shards, mesh=torus, in_specs=placed, out_specs=P(CLIP, "row", None), check_vma=False
    )
```

time: 70.4 us -> 61.6 us (0.88)
  Pallas kernels: 26.4 us -> 21.4 us
  waiting for transfers between devices: 10.2 us -> 8.25 us
  local copies, waits for them, and re-layouts: 4.08 us -> 3.09 us
  starting transfers between devices: 26.3 us -> 25.5 us
    pallas_call x3 -> x4, Pallas kernels: 24.2 us -> 18.9 us  [the longest x3 13.3 us: attend_remote(): pl.pallas_call(functools.partial(remote_kernel, places), out_shape=ACC, i...]
    ppermute x7, waiting for transfers between devices: 4.36 us -> 2.5 us  [plane_shift(): return lax.ppermute(block, PLANE, route)]
    select_n x0 -> x1, other arithmetic: none -> 1.46 us  [shards(): jnp.where((slot >= caps[0]) & (entry >= KVH * HD), jnp.bfloat16(DEAD), mine)]
    sub x1 -> x0, other arithmetic: 0.8 us -> none  [limits(): from_y = (y - jnp.where(role == 0, db, da)) % YS]
    ppermute x5, starting transfers between devices: 6.4 us -> 5.6 us  [other_core(): return lax.ppermute(block, 'row', [(0, 1), (1, 0)])]
    broadcast_in_dim x1 -> x0, other arithmetic: 0.8 us -> none  [shards(): copies = jnp.broadcast_to(mine[None], (ZS, HALF, 4 * HD))]
    unnamed x4 -> x6, local copies, waits for them, and re-layouts: 2.13 us -> 2.14 us
  transfers between devices with their start and end apart: 14 -> 14, of which waited for: 3 -> 2; matrix products, arithmetic and copies ran while one was open for 3% -> 2% of each run, Pallas kernels for 26% -> 26%
where the time goes in v2:
time: 61.6 us; the launch traced here: 61.3 us
  starting transfers between devices  25.5 us (41%)
  Pallas kernels  21.4 us (35%)
  waiting for transfers between devices  8.25 us (13%)
  local copies, waits for them, and re-layouts  3.09 us (5%)
  other arithmetic  1.62 us (3%)
  between operations  1.46 us (2%)
    pallas_call x3, Pallas kernels, attend_remote(): pl.pallas_call(functools.partial(remote_kernel, places), out_shape=ACC, i...  13.3 us
    ppermute x7, starting transfers between devices, plane_shift(): return lax.ppermute(block, PLANE, route)  9.81 us
    all_to_all x1, starting transfers between devices, shards(): column = lax.all_to_all(copies, 'z', 0, 0, tiled=True)  9.01 us
    all_to_all x1, waiting for transfers between devices, shards(): column = lax.all_to_all(copies, 'z', 0, 0, tiled=True)  5.73 us
    ppermute x5, starting transfers between devices, other_core(): return lax.ppermute(block, 'row', [(0, 1), (1, 0)])  5.6 us
    pallas_call x1, Pallas kernels, attend_last(): pl.pallas_call(functools.partial(last_kernel, places, new), out_shape=jax...  5.59 us
    ppermute x7, waiting for transfers between devices, plane_shift(): return lax.ppermute(block, PLANE, route)  2.5 us
    pallas_call x1, Pallas kernels, attend_local(): pl.pallas_call(local_kernel, out_shape=(jax.ShapeDtypeStruct((KVH, ROWS,...  2.5 us
  transfers between devices with their start and end apart: 14, of which 2 were waited for; matrix products, arithmetic and copies ran while one was open for 2% of the time, Pallas kernels for 26%

profile of v2, /device:TPU:1, one launch (start us, length us, event | category | flops | bytes accessed | tf_op | source)
XLA Modules:
  0.0 61.3 jit_solution(15134165186774787776)
XLA Ops:
  0.7 1.5 %and_select_fusion = bf16[8,16,512]{2,1,0:T(8,128)(2,1)} fusion(pred[512]{0:T(512)(128)(4,1)S(1)} %iota_compare_fusion, pred[16]{0:T(512)(128)(4,1)S(1)} %add_compare_fusion, bf16[16,512]{1,0:T(8,128)(2,1)} %bitcast.34), kind=kLoop, calls=%fused_computation.1 | loop fusion | flops 131072 | bytes 147984 | tf_op jit(solution)/shard_map/jit(_where)/select_n | solution.py:310
  2.1 9.0 %all-to-all-start = ((bf16[8,16,512]{2,1,0:T(8,128)(2,1)}), bf16[8,16,512]{2,1,0:T(8,128)(2,1)S(1)}, u32[]{:S(2)}, u32[]{:S(2)}) async-start(bf16[8,16,512]{2,1,0:T(8,128)(2,1)} %and_select_fusion), calls=%async_computation | async-start | bytes 262144 | tf_op jit(solution)/shard_map/all_to_all | solution.py:312
  11.1 0.9 %slice.9 = bf16[128,512]{1,0:T(8,128)(2,1)S(1)} slice(bf16[256,512]{1,0:T(8,128)(2,1)} %bitcast.26), slice={[128:256], [0:512]} | slice | bytes 262144 | tf_op jit(solution)/shard_map/slice | solution.py:313
  12.1 1.0 %collective-permute-start.3 = (bf16[128,512]{1,0:T(8,128)(2,1)S(1)}, bf16[128,512]{1,0:T(8,128)(2,1)S(1)}, u32[]{:S(2)}, u32[]{:S(2)}) collective-permute-start(bf16[128,512]{1,0:T(8,128)(2,1)S(1)} %slice.9), channel_id=1, source_target_pairs={{0,1},{1,0},{2,3},{3,2},{4,5},{5,4},{6,7},{7,6},{8,9},{9,8},{10,11... | collective-permute-start | bytes 393224 | tf_op jit(solution)/shard_map/ppermute | solution.py:313
  13.1 0.1 pad_add_fusion.ids
  13.2 5.7 %all-to-all-done = bf16[8,16,512]{2,1,0:T(8,128)(2,1)S(1)} async-done(((bf16[8,16,512]{2,1,0:T(8,128)(2,1)}), bf16[8,16,512]{2,1,0:T(8,128)(2,1)S(1)}, u32[]{:S(2)}, u32[]{:S(2)}) %all-to-all-start) | async-done | bytes 131104 | tf_op jit(solution)/shard_map/all_to_all | solution.py:312
  18.9 1.3 %collective-permute-start = (bf16[8,16,512]{2,1,0:T(8,128)(2,1)S(1)}, bf16[8,16,512]{2,1,0:T(8,128)(2,1)S(1)}, u32[]{:S(2)}, u32[]{:S(2)}) collective-permute-start(bf16[8,16,512]{2,1,0:T(8,128)(2,1)S(1)} %all-to-all-done), channel_id=1, source_target_pairs={{0,2},{1,9},{2,4},{3,11},{4,6},{5,13},{6,0},{7,15},{8,10},{9,17},{... | collective-permute-start | bytes 393224 | tf_op jit(solution)/shard_map/ppermute | solution.py:46
  20.2 1.4 %collective-permute-start.1 = (bf16[8,16,512]{2,1,0:T(8,128)(2,1)S(1)}, bf16[8,16,512]{2,1,0:T(8,128)(2,1)S(1)}, u32[]{:S(2)}, u32[]{:S(2)}) collective-permute-start(bf16[8,16,512]{2,1,0:T(8,128)(2,1)S(1)} %all-to-all-done), channel_id=1, source_target_pairs={{0,6},{1,25},{2,0},{3,27},{4,2},{5,29},{6,4},{7,31},{8,14},{9,1},{... | collective-permute-start | bytes 393224 | tf_op jit(solution)/shard_map/ppermute | solution.py:46
  21.7 1.6 %collective-permute-start.2 = (bf16[8,16,512]{2,1,0:T(8,128)(2,1)S(1)}, bf16[8,16,512]{2,1,0:T(8,128)(2,1)S(1)}, u32[]{:S(2)}, u32[]{:S(2)}) collective-permute-start(bf16[8,16,512]{2,1,0:T(8,128)(2,1)S(1)} %all-to-all-done), channel_id=1, source_target_pairs={{0,4},{1,17},{2,6},{3,19},{4,0},{5,21},{6,2},{7,23},{8,12},{9,25},... | collective-permute-start | bytes 393224 | tf_op jit(solution)/shard_map/ppermute | solution.py:46
  23.3 0.0 collective-permute-done.3.rim_ref
  23.3 0.0 copy-start
  23.3 0.9 %copy-done = bf16[1,256,512]{2,1,0:T(8,128)(2,1)S(1)} copy-done((bf16[1,256,512]{2,1,0:T(8,128)(2,1)S(1)}, bf16[1,256,512]{2,1,0:T(8,128)(2,1)}, u32[]{:S(2)}) %copy-start) | copy-done | bytes 262168
  24.2 0.0 copy-start.2
  24.3 1.2 %copy-done.2 = bf16[1,256,1792]{2,1,0:T(8,128)(2,1)S(1)} copy-done((bf16[1,256,1792]{2,1,0:T(8,128)(2,1)S(1)}, bf16[1,256,1792]{2,1,0:T(8,128)(2,1)}, u32[]{:S(2)}) %copy-start.2) | copy-done | bytes 917528
  25.4 2.5 %local.1 = (bf16[2,1792,256]{2,1,0:T(8,128)(2,1)S(1)}, f32[2,1792,256]{2,1,0:T(8,128)S(1)}) custom-call(s32[4]{0:T(128)S(1)} %pad_add_fusion.ids, bf16[256,1792]{1,0:T(8,128)(2,1)S(1)} %bitcast.29, bf16[128,512]{1,0:T(8,128)(2,1)S(1)} %collective-permute-done.3.rim_ref, bf16[256,512]{1,0:T(8,128)(2,1)S(1)} %bitcast.27), custom_call_target="tpu_custom_call" | custom-call | flops 3758096384 | bytes 1048576 | tf_op jit(solution)/shard_map/local/pallas_call | solution.py:264
  27.9 0.0 collective-permute-done
  27.9 0.0 collective-permute-done.1
  28.0 0.0 collective-permute-done.2
  28.0 0.1 pad_maximum_fusion
  28.0 3.0 %collective-permute-start.6 = (bf16[512,512]{1,0:T(8,128)(2,1)S(1)}, bf16[512,512]{1,0:T(8,128)(2,1)S(1)}, u32[]{:S(2)}, u32[]{:S(2)}) collective-permute-start(bf16[512,512]{1,0:T(8,128)(2,1)S(1)} %bitcast.21), channel_id=1, source_target_pairs={{0,1},{1,0},{2,3},{3,2},{4,5},{5,4},{6,7},{7,6},{8,9},{9,8},{10,11... | collective-permute-start | bytes 1572872 | tf_op jit(solution)/shard_map/ppermute | solution.py:50
  31.1 0.3 collective-permute-start.4
  31.4 2.4 %collective-permute-start.5 = (bf16[512,512]{1,0:T(8,128)(2,1)S(1)}, bf16[512,512]{1,0:T(8,128)(2,1)S(1)}, u32[]{:S(2)}, u32[]{:S(2)}) collective-permute-start(bf16[512,512]{1,0:T(8,128)(2,1)S(1)} %bitcast.23), channel_id=1, source_target_pairs={{0,24},{1,7},{2,26},{3,1},{4,28},{5,3},{6,30},{7,5},{8,0},{9,15},{... | collective-permute-start | bytes 1572872 | tf_op jit(solution)/shard_map/ppermute | solution.py:46
  33.8 0.0 collective-permute-done.6.rest_1_.rest_5_
  33.8 4.4 %remote.3.acc_ref = f32[2,1792,256]{2,1,0:T(8,128)S(1)} custom-call(s32[4]{0:T(128)S(1)} %pad_add_fusion.ids, bf16[2,1792,256]{2,1,0:T(8,128)(2,1)S(1)} %get-tuple-element.29.qa_ref, f32[2,1792,256]{2,1,0:T(8,128)S(1)} %get-tuple-element.34.acc_ref, bf16[512,512]{1,0:T(8,128)(2,1)S(1)} %bitcast.24, bf16[512,512]{1,0:T(8,128)(2,1)S(1)} %collective-permute-done.6.rest_1_.rest_5_), custom_call_target="tpu_custom_call" | custom-call | flops 7516192768 | bytes 1048576 | tf_op jit(solution)/shard_map/remote/pallas_call | solution.py:278
  38.1 2.5 %collective-permute-done.4.rest_0_.rest_6_ = bf16[512,512]{1,0:T(8,128)(2,1)S(1)} collective-permute-done((bf16[512,512]{1,0:T(8,128)(2,1)S(1)}, bf16[512,512]{1,0:T(8,128)(2,1)S(1)}, u32[]{:S(2)}, u32[]{:S(2)}) %collective-permute-start.4) | collective-permute-done | bytes 524320 | tf_op jit(solution)/shard_map/ppermute | solution.py:46
  40.6 0.0 collective-permute-done.5.rest_0_.rest_8_
  40.6 1.3 %collective-permute-start.9 = (bf16[512,512]{1,0:T(8,128)(2,1)S(1)}, bf16[512,512]{1,0:T(8,128)(2,1)S(1)}, u32[]{:S(2)}, u32[]{:S(2)}) collective-permute-start(bf16[512,512]{1,0:T(8,128)(2,1)S(1)} %collective-permute-done.4.rest_0_.rest_6_), channel_id=1, source_target_pairs={{0,1},{1,0},{2,3},{3,2},{4,5},{5,4},{6,7},{7,6},{8,9},{9,8},{10,11... | collective-permute-start | bytes 1572872 | tf_op jit(solution)/shard_map/ppermute | solution.py:50
  42.6 0.1 collective-permute-start.10
  42.7 0.4 collective-permute-start.7
  43.1 2.4 %collective-permute-start.8 = (bf16[256,512]{1,0:T(8,128)(2,1)S(1)}, bf16[256,512]{1,0:T(8,128)(2,1)S(1)}, u32[]{:S(2)}, u32[]{:S(2)}) collective-permute-start(bf16[256,512]{1,0:T(8,128)(2,1)S(1)} %slice.11), channel_id=1, source_target_pairs={{0,24},{1,7},{2,26},{3,1},{4,28},{5,3},{6,30},{7,5},{8,0},{9,15},{... | collective-permute-start | bytes 786440 | tf_op jit(solution)/shard_map/ppermute | solution.py:46
  45.5 0.0 collective-permute-done.9.rest_1_.rest_7_
  45.5 4.5 %remote.4.acc_ref = f32[2,1792,256]{2,1,0:T(8,128)S(1)} custom-call(s32[4]{0:T(128)S(1)} %pad_add_fusion.ids, bf16[2,1792,256]{2,1,0:T(8,128)(2,1)S(1)} %get-tuple-element.29.qa_ref, f32[2,1792,256]{2,1,0:T(8,128)S(1)} %remote.3.acc_ref, bf16[512,512]{1,0:T(8,128)(2,1)S(1)} %collective-permute-done.4.rest_0_.rest_6_, ...), custom_call_target="tpu_custom_call" | custom-call | flops 7516192768 | bytes 1048576 | tf_op jit(solution)/shard_map/remote/pallas_call | solution.py:278
  50.0 0.0 copy-start.1
  50.1 0.0 collective-permute-done.7.rest_0_
  50.1 0.0 collective-permute-done.8.rest_2_
  50.1 1.1 %collective-permute-start.11 = (bf16[256,512]{1,0:T(8,128)(2,1)S(1)}, bf16[256,512]{1,0:T(8,128)(2,1)S(1)}, u32[]{:S(2)}, u32[]{:S(2)}) collective-permute-start(bf16[256,512]{1,0:T(8,128)(2,1)S(1)} %collective-permute-done.7.rest_0_), channel_id=1, source_target_pairs={{0,1},{1,0},{2,3},{3,2},{4,5},{5,4},{6,7},{7,6},{8,9},{9,8},{10,11... | collective-permute-start | bytes 786440 | tf_op jit(solution)/shard_map/ppermute | solution.py:50
  51.2 0.1 collective-permute-start.12
  51.2 0.0 collective-permute-done.10.rest_1_.rest_9_
  51.2 4.4 %remote.5.acc_ref = f32[2,1792,256]{2,1,0:T(8,128)S(1)} custom-call(s32[4]{0:T(128)S(1)} %pad_add_fusion.ids, bf16[2,1792,256]{2,1,0:T(8,128)(2,1)S(1)} %get-tuple-element.29.qa_ref, f32[2,1792,256]{2,1,0:T(8,128)S(1)} %remote.4.acc_ref, bf16[512,512]{1,0:T(8,128)(2,1)S(1)} %collective-permute-done.5.rest_0_.rest_8_, ...), custom_call_target="tpu_custom_call" | custom-call | flops 7516192768 | bytes 1048576 | tf_op jit(solution)/shard_map/remote/pallas_call | solution.py:278
  55.7 0.0 collective-permute-done.11.rest_1_
  55.7 0.0 collective-permute-done.12.rest_3_
  55.7 0.0 copy-done.1
  55.7 5.6 %last.1 = bf16[256,1792]{1,0:T(8,128)(2,1)} custom-call(s32[4]{0:T(128)S(1)} %pad_add_fusion.ids, s32[1]{0:T(128)S(6)} %copy.9.lengths, bf16[2,1792,256]{2,1,0:T(8,128)(2,1)S(1)} %get-tuple-element.29.qa_ref, bf16[128,512]{1,0:T(8,128)(2,1)S(1)} %collective-permute-done.3.rim_ref, bf16[256,512]{1,0:T(8,128)(2,1)S(1)} %bitcast.28, ...), custom_call_target="tpu_custom_call" | custom-call | flops 30064771072 | bytes 1048576 | tf_op jit(solution)/shard_map/last/pallas_call | solution.py:292
  (4 shorter events, 0.1 us)
Async XLA Ops:
  2.1 16.8 %all-to-all-start = ((bf16[8,16,512]{2,1,0:T(8,128)(2,1)}), bf16[8,16,512]{2,1,0:T(8,128)(2,1)S(1)}, u32[]{:S(2)}, u32[]{:S(2)}) async-start(bf16[8,16,512]{2,1,0:T(8,128)(2,1)} %and_select_fusion), calls=%async_computation | async-start | bytes 262144 | tf_op jit(solution)/shard_map/all_to_all | solution.py:312
  12.1 11.2 %collective-permute-start.3 = (bf16[128,512]{1,0:T(8,128)(2,1)S(1)}, bf16[128,512]{1,0:T(8,128)(2,1)S(1)}, u32[]{:S(2)}, u32[]{:S(2)}) collective-permute-start(bf16[128,512]{1,0:T(8,128)(2,1)S(1)} %slice.9), channel_id=1, source_target_pairs={{0,1},{1,0},{2,3},{3,2},{4,5},{5,4},{6,7},{7,6},{8,9},{9,8},{10,11... | collective-permute-start | bytes 393224 | tf_op jit(solution)/shard_map/ppermute | solution.py:313
  18.9 9.0 %collective-permute-start = (bf16[8,16,512]{2,1,0:T(8,128)(2,1)S(1)}, bf16[8,16,512]{2,1,0:T(8,128)(2,1)S(1)}, u32[]{:S(2)}, u32[]{:S(2)}) collective-permute-start(bf16[8,16,512]{2,1,0:T(8,128)(2,1)S(1)} %all-to-all-done), channel_id=1, source_target_pairs={{0,2},{1,9},{2,4},{3,11},{4,6},{5,13},{6,0},{7,15},{8,10},{9,17},{... | collective-permute-start | bytes 393224 | tf_op jit(solution)/shard_map/ppermute | solution.py:46
  20.2 7.7 %collective-permute-start.1 = (bf16[8,16,512]{2,1,0:T(8,128)(2,1)S(1)}, bf16[8,16,512]{2,1,0:T(8,128)(2,1)S(1)}, u32[]{:S(2)}, u32[]{:S(2)}) collective-permute-start(bf16[8,16,512]{2,1,0:T(8,128)(2,1)S(1)} %all-to-all-done), channel_id=1, source_target_pairs={{0,6},{1,25},{2,0},{3,27},{4,2},{5,29},{6,4},{7,31},{8,14},{9,1},{... | collective-permute-start | bytes 393224 | tf_op jit(solution)/shard_map/ppermute | solution.py:46
  21.7 6.3 %collective-permute-start.2 = (bf16[8,16,512]{2,1,0:T(8,128)(2,1)S(1)}, bf16[8,16,512]{2,1,0:T(8,128)(2,1)S(1)}, u32[]{:S(2)}, u32[]{:S(2)}) collective-permute-start(bf16[8,16,512]{2,1,0:T(8,128)(2,1)S(1)} %all-to-all-done), channel_id=1, source_target_pairs={{0,4},{1,17},{2,6},{3,19},{4,0},{5,21},{6,2},{7,23},{8,12},{9,25},... | collective-permute-start | bytes 393224 | tf_op jit(solution)/shard_map/ppermute | solution.py:46
  23.3 1.0 %copy-start = (bf16[1,256,512]{2,1,0:T(8,128)(2,1)S(1)}, bf16[1,256,512]{2,1,0:T(8,128)(2,1)}, u32[]{:S(2)}) copy-start(bf16[1,256,512]{2,1,0:T(8,128)(2,1)} %param.6) | copy-start | bytes 786436
  24.2 1.2 %copy-start.2 = (bf16[1,256,1792]{2,1,0:T(8,128)(2,1)S(1)}, bf16[1,256,1792]{2,1,0:T(8,128)(2,1)}, u32[]{:S(2)}) copy-start(bf16[1,256,1792]{2,1,0:T(8,128)(2,1)} %param.5) | copy-start | bytes 2752516
  28.0 5.7 %collective-permute-start.6 = (bf16[512,512]{1,0:T(8,128)(2,1)S(1)}, bf16[512,512]{1,0:T(8,128)(2,1)S(1)}, u32[]{:S(2)}, u32[]{:S(2)}) collective-permute-start(bf16[512,512]{1,0:T(8,128)(2,1)S(1)} %bitcast.21), channel_id=1, source_target_pairs={{0,1},{1,0},{2,3},{3,2},{4,5},{5,4},{6,7},{7,6},{8,9},{9,8},{10,11... | collective-permute-start | bytes 1572872 | tf_op jit(solution)/shard_map/ppermute | solution.py:50
  31.1 9.5 %collective-permute-start.4 = (bf16[512,512]{1,0:T(8,128)(2,1)S(1)}, bf16[512,512]{1,0:T(8,128)(2,1)S(1)}, u32[]{:S(2)}, u32[]{:S(2)}) collective-permute-start(bf16[512,512]{1,0:T(8,128)(2,1)S(1)} %bitcast.22), channel_id=1, source_target_pairs={{0,8},{1,3},{2,10},{3,5},{4,12},{5,7},{6,14},{7,1},{8,16},{9,11},{... | collective-permute-start | bytes 1572872 | tf_op jit(solution)/shard_map/ppermute | solution.py:46
  31.4 9.2 %collective-permute-start.5 = (bf16[512,512]{1,0:T(8,128)(2,1)S(1)}, bf16[512,512]{1,0:T(8,128)(2,1)S(1)}, u32[]{:S(2)}, u32[]{:S(2)}) collective-permute-start(bf16[512,512]{1,0:T(8,128)(2,1)S(1)} %bitcast.23), channel_id=1, source_target_pairs={{0,24},{1,7},{2,26},{3,1},{4,28},{5,3},{6,30},{7,5},{8,0},{9,15},{... | collective-permute-start | bytes 1572872 | tf_op jit(solution)/shard_map/ppermute | solution.py:46
  40.6 4.9 %collective-permute-start.9 = (bf16[512,512]{1,0:T(8,128)(2,1)S(1)}, bf16[512,512]{1,0:T(8,128)(2,1)S(1)}, u32[]{:S(2)}, u32[]{:S(2)}) collective-permute-start(bf16[512,512]{1,0:T(8,128)(2,1)S(1)} %collective-permute-done.4.rest_0_.rest_6_), channel_id=1, source_target_pairs={{0,1},{1,0},{2,3},{3,2},{4,5},{5,4},{6,7},{7,6},{8,9},{9,8},{10,11... | collective-permute-start | bytes 1572872 | tf_op jit(solution)/shard_map/ppermute | solution.py:50
  42.6 8.6 %collective-permute-start.10 = (bf16[512,512]{1,0:T(8,128)(2,1)S(1)}, bf16[512,512]{1,0:T(8,128)(2,1)S(1)}, u32[]{:S(2)}, u32[]{:S(2)}) collective-permute-start(bf16[512,512]{1,0:T(8,128)(2,1)S(1)} %collective-permute-done.5.rest_0_.rest_8_), channel_id=1, source_target_pairs={{0,1},{1,0},{2,3},{3,2},{4,5},{5,4},{6,7},{7,6},{8,9},{9,8},{10,11... | collective-permute-start | bytes 1572872 | tf_op jit(solution)/shard_map/ppermute | solution.py:50
  42.7 7.3 %collective-permute-start.7 = (bf16[256,512]{1,0:T(8,128)(2,1)S(1)}, bf16[256,512]{1,0:T(8,128)(2,1)S(1)}, u32[]{:S(2)}, u32[]{:S(2)}) collective-permute-start(bf16[256,512]{1,0:T(8,128)(2,1)S(1)} %slice.10), channel_id=1, source_target_pairs={{0,8},{1,3},{2,10},{3,5},{4,12},{5,7},{6,14},{7,1},{8,16},{9,11},{... | collective-permute-start | bytes 786440 | tf_op jit(solution)/shard_map/ppermute | solution.py:46
  43.1 6.9 %collective-permute-start.8 = (bf16[256,512]{1,0:T(8,128)(2,1)S(1)}, bf16[256,512]{1,0:T(8,128)(2,1)S(1)}, u32[]{:S(2)}, u32[]{:S(2)}) collective-permute-start(bf16[256,512]{1,0:T(8,128)(2,1)S(1)} %slice.11), channel_id=1, source_target_pairs={{0,24},{1,7},{2,26},{3,1},{4,28},{5,3},{6,30},{7,5},{8,0},{9,15},{... | collective-permute-start | bytes 786440 | tf_op jit(solution)/shard_map/ppermute | solution.py:46
  50.0 5.6 %copy-start.1 = (bf16[1,256,512]{2,1,0:T(8,128)(2,1)S(1)}, bf16[1,256,512]{2,1,0:T(8,128)(2,1)}, u32[]{:S(2)}) copy-start(bf16[1,256,512]{2,1,0:T(8,128)(2,1)} %param.6) | copy-start | bytes 786436
  50.1 5.6 %collective-permute-start.11 = (bf16[256,512]{1,0:T(8,128)(2,1)S(1)}, bf16[256,512]{1,0:T(8,128)(2,1)S(1)}, u32[]{:S(2)}, u32[]{:S(2)}) collective-permute-start(bf16[256,512]{1,0:T(8,128)(2,1)S(1)} %collective-permute-done.7.rest_0_), channel_id=1, source_target_pairs={{0,1},{1,0},{2,3},{3,2},{4,5},{5,4},{6,7},{7,6},{8,9},{9,8},{10,11... | collective-permute-start | bytes 786440 | tf_op jit(solution)/shard_map/ppermute | solution.py:50
  51.2 4.5 %collective-permute-start.12 = (bf16[256,512]{1,0:T(8,128)(2,1)S(1)}, bf16[256,512]{1,0:T(8,128)(2,1)S(1)}, u32[]{:S(2)}, u32[]{:S(2)}) collective-permute-start(bf16[256,512]{1,0:T(8,128)(2,1)S(1)} %collective-permute-done.8.rest_2_), channel_id=1, source_target_pairs={{0,1},{1,0},{2,3},{3,2},{4,5},{5,4},{6,7},{7,6},{8,9},{9,8},{10,11... | collective-permute-start | bytes 786440 | tf_op jit(solution)/shard_map/ppermute | solution.py:50

commit v3 on v2

--- a/solution.py
+++ b/solution.py
@@ -26,8 +26,8 @@
 CLOSED = -1e30
 LARGE = 1e30
 DA = (0, 1, 3, 2)
+SMEM = pl.BlockSpec(memory_space=pltpu.SMEM)
 VMEM = pl.BlockSpec(memory_space=pltpu.VMEM)
-SMEM = pl.BlockSpec(memory_space=pltpu.SMEM)
 NT = (((1,), (1,)), ((), ()))
 BQ = 896
 BK = 256
@@ -62,14 +62,14 @@
     return (jnp.concatenate([rim_ref[:, columns], own[:WINDOW]], axis=0), own)
 
 
-def local_kernel(ids, q_hbm, rim_ref, own_ref, qa_ref, acc_ref, q_ref, sems):
+def local_kernel(q_hbm, rim_ref, own_ref, qa_ref, acc_ref, q_ref, sems):
     wide = GROUP * HD
     copies = [
         pltpu.make_async_copy(q_hbm.at[:, pl.ds(h * wide, wide)], q_ref.at[h], sems.at[h]) for h in range(KVH)
     ]
     for copy in copies:
         copy.start()
-    masks = band_masks(ids)
+    masks = band_masks(own_place())
     lane = lax.broadcasted_iota(jnp.int32, (WINDOW, HD), 1)
     ones = jnp.ones((2 * WINDOW, HD), jnp.bfloat16)
     for h in range(KVH):
@@ -118,65 +118,76 @@
             at += BK
 
 
-def key_tiles(chunks, upper):
+def key_tiles(chunks, level):
     at = 0
-    found = []
+    pieces = []
     for ref, _, _, base in chunks:
         for b in range(ref.shape[0] // BK):
-            if upper or base + b == 0:
-                found.append((ref, b * BK, at))
+            if level == 3 or base + b == 0:
+                pieces.append((ref, b * BK, at, BK if level == 3 else BK >> (2 - level)))
             at += BK
-    return found
+    each = BK // pieces[0][3]
+    return [pieces[n : n + each] for n in range(0, len(pieces), each)]
 
 
 def head_columns(j):
+    if isinstance(j, int):
+        return slice(j * HD, (j + 1) * HD)
     return pl.ds(pl.multiple_of(j * HD, HD), HD)
 
 
-def scores(q, ref, start, at, h, extra):
-    key = jnp.concatenate([ref[start : start + BK, head_columns(h)], extra[at : at + BK, :]], axis=1)
+def scores(q, tile, h, extra):
+    key = [ref[start : start + size, head_columns(h)] for ref, start, _, size in tile]
+    beside = [extra[at : at + size, :] for _, _, at, size in tile]
+    key = jnp.concatenate([jnp.concatenate(key, axis=0), jnp.concatenate(beside, axis=0)], axis=1)
     return lax.dot_general(q, key, NT, preferred_element_type=jnp.float32)
 
 
-def weighted(p, ref, start, h):
-    ones = jnp.ones((BK, HD), jnp.bfloat16)
-    value = jnp.concatenate([ref[start : start + BK, head_columns(KVH + h)], ones], axis=1)
+def weighted(p, tile, h):
+    value = [ref[start : start + size, head_columns(KVH + h)] for ref, start, _, size in tile]
+    value = jnp.concatenate(value, axis=0)
+    value = jnp.concatenate([value, jnp.ones((value.shape[0], HD), jnp.bfloat16)], axis=1)
     return jnp.dot(p.astype(jnp.bfloat16), value, preferred_element_type=jnp.float32)
 
 
 def accumulate(acc, q, tiles, h, extra):
-    for ref, start, at in tiles:
-        p = jnp.exp2(scores(q, ref, start, at, h, extra) * RATE)
-        acc = acc + weighted(p, ref, start, h)
+    for tile in tiles:
+        acc = acc + weighted(jnp.exp2(scores(q, tile, h, extra) * RATE), tile, h)
     return acc
 
 
 def by_height(ids, run):
-    high = ids[1] >= ZS // 2
-    pl.when(high)(lambda: run(True))
-    pl.when(jnp.logical_not(high))(lambda: run(False))
+    z = ids[1]
+    pl.when(z == 0)(lambda: run(0))
+    pl.when(z == 1)(lambda: run(1))
+    pl.when((z >= 2) & (z < 4))(lambda: run(2))
+    pl.when(z >= 4)(lambda: run(3))
 
 
 def each_block(body):
-    blocks = ROWS // BQ
-
-    def step(n, carry):
-        body(n // blocks, lax.rem(n, blocks))
+    def step(h, carry):
+        for i in range(ROWS // BQ):
+            body(h, i)
         return carry
 
-    lax.fori_loop(0, KVH * blocks, step, 0)
-
-
-def remote_kernel(places, ids, qa_ref, acc_ref, *rest):
+    lax.fori_loop(0, KVH, step, 0)
+
+
+def own_place():
+    return [lax.axis_index(name) for name in ("row", "z", "y", "x")]
+
+
+def remote_kernel(places, qa_ref, acc_ref, *rest):
     refs, (out_ref, extra) = rest[: len(places)], rest[len(places) :]
     chunks = [(ref, *place) for ref, place in zip(refs, places)]
+    ids = own_place()
     build_extra(ids, chunks, extra)
 
-    def run(upper):
-        tiles = key_tiles(chunks, upper)
+    def run(level):
+        tiles = key_tiles(chunks, level)
 
         def body(h, i):
-            rows = pl.ds(i * BQ, BQ)
+            rows = slice(i * BQ, (i + 1) * BQ)
             out_ref[h, rows, :] = accumulate(acc_ref[h, rows, :], qa_ref[h, rows, :], tiles, h, extra)
 
         each_block(body)
@@ -184,27 +195,27 @@
     by_height(ids, run)
 
 
-def last_kernel(places, new, ids, lengths, qa_ref, rim_ref, own_ref, acc_ref, *rest):
+def last_kernel(places, new, room_ref, qa_ref, rim_ref, own_ref, acc_ref, *rest):
     refs, (out_ref, extra, worst) = rest[: len(places)], rest[len(places) :]
     chunks = [(ref, *place) for ref, place in zip(refs, places)]
+    ids = own_place()
     build_extra(ids, chunks[:new], extra)
-    count = lengths[0] - ids[0] * TOKENS
     token = lax.broadcasted_iota(jnp.int32, (WINDOW, HD), 0)
+    room = room_ref[0] - ids[0] * TOKENS
     worst[...] = jnp.zeros_like(worst)
 
     def finish(h, piece, acc):
         result = acc[:, :HD] / acc[:, HD:]
-        first = lax.rem(piece, 2) * WINDOW
-        column = (h * GROUP + piece // 2) * HD
-        present = token + first < count
-        where = (pl.ds(pl.multiple_of(first, WINDOW), WINDOW), pl.ds(pl.multiple_of(column, HD), HD))
-        out_ref[where] = jnp.where(present, result, 0.0).astype(jnp.bfloat16)
-
-    def run(upper):
-        tiles = key_tiles(chunks[:new], upper)
+        first = piece % 2 * WINDOW
+        present = token + first < room
+        rows = slice(first, first + WINDOW) if isinstance(piece, int) else pl.ds(pl.multiple_of(first, WINDOW), WINDOW)
+        out_ref[rows, head_columns(h * GROUP + piece // 2)] = jnp.where(present, result, 0.0).astype(jnp.bfloat16)
+
+    def run(level):
+        tiles = key_tiles(chunks[:new], level)
 
         def body(h, i):
-            rows = pl.ds(i * BQ, BQ)
+            rows = slice(i * BQ, (i + 1) * BQ)
             acc = accumulate(acc_ref[h, rows, :], qa_ref[h, rows, :], tiles, h, extra)
             largest = worst[...]
             for k in range(BQ // WINDOW):
@@ -220,7 +231,7 @@
     @pl.when(jnp.logical_not(jnp.max(worst[...]) < LARGE))
     def _():
         build_extra(ids, chunks, extra)
-        tiles = key_tiles(chunks, True)
+        tiles = key_tiles(chunks, 3)
         masks = band_masks(ids)
 
         def redo(n, carry):
@@ -228,8 +239,8 @@
             rows = pl.ds(piece * WINDOW, WINDOW)
             q = qa_ref[h, rows, :]
             top = jnp.zeros((WINDOW, 1), jnp.float32)
-            for ref, start, at in tiles:
-                s = scores(q, ref, start, at, h, extra)
+            for tile in tiles:
+                s = scores(q, tile, h, extra)
                 top = jnp.maximum(top, jnp.max(s, axis=1, keepdims=True))
             first = lax.rem(piece, 2) == 0
             keys = band_frames(rim_ref, own_ref, head_columns(h))
@@ -241,9 +252,9 @@
             shift = q[:, HD : HD + 1].astype(jnp.float32) + top
             p = jnp.where(mask, jnp.exp2((s - shift) * RATE), 0.0)
             acc = jnp.dot(p.astype(jnp.bfloat16), value, preferred_element_type=jnp.float32)
-            for ref, start, at in tiles:
-                p = jnp.exp2((scores(q, ref, start, at, h, extra) - top) * RATE)
-                acc = acc + weighted(p, ref, start, h)
+            for tile in tiles:
+                p = jnp.exp2((scores(q, tile, h, extra) - top) * RATE)
+                acc = acc + weighted(p, tile, h)
             finish(h, piece, acc)
             return carry
 
@@ -260,50 +271,49 @@
 ACC = jax.ShapeDtypeStruct((KVH, ROWS, 2 * HD), jnp.float32)
 
 
-def attend_local(ids, q, rim, own):
+def attend_local(q, rim, own):
     return pl.pallas_call(
         local_kernel,
         out_shape=(jax.ShapeDtypeStruct((KVH, ROWS, 2 * HD), jnp.bfloat16), ACC),
-        in_specs=[SMEM, pl.BlockSpec(memory_space=pltpu.HBM), VMEM, VMEM],
+        in_specs=[pl.BlockSpec(memory_space=pltpu.HBM), VMEM, VMEM],
         out_specs=(VMEM, VMEM),
         scratch_shapes=[pltpu.VMEM((KVH, TOKENS, GROUP * HD), jnp.bfloat16), pltpu.SemaphoreType.DMA((KVH,))],
         compiler_params=PARAMS,
         cost_estimate=cost(512),
         name="local",
-    )(ids, q, rim, own)
-
-
-def attend_remote(ids, qa, acc, chunks, places):
+    )(q, rim, own)
+
+
+def attend_remote(qa, acc, chunks, places):
     keys = sum(c.shape[0] for c in chunks)
     return pl.pallas_call(
         functools.partial(remote_kernel, places),
         out_shape=ACC,
-        in_specs=[SMEM] + [VMEM] * (2 + len(chunks)),
+        in_specs=[VMEM] * (2 + len(chunks)),
         out_specs=VMEM,
         scratch_shapes=[pltpu.VMEM((keys, HD), jnp.bfloat16)],
         compiler_params=PARAMS,
         cost_estimate=cost(keys),
         name="remote",
-    )(ids, qa, acc, *chunks)
-
-
-def attend_last(ids, lengths, qa, rim, own, acc, chunks, places, new):
+    )(qa, acc, *chunks)
+
+
+def attend_last(room, qa, rim, own, acc, chunks, places, new):
     keys = sum(c.shape[0] for c in chunks)
     return pl.pallas_call(
         functools.partial(last_kernel, places, new),
         out_shape=jax.ShapeDtypeStruct((TOKENS, KVH * GROUP * HD), jnp.bfloat16),
-        in_specs=[SMEM] * 2 + [VMEM] * (4 + len(chunks)),
+        in_specs=[SMEM] + [VMEM] * (4 + len(chunks)),
         out_specs=VMEM,
         scratch_shapes=[pltpu.VMEM((keys, HD), jnp.bfloat16), pltpu.VMEM((WINDOW, HD), jnp.float32)],
         compiler_params=PARAMS,
         cost_estimate=cost(keys),
         name="last",
-    )(ids, lengths, qa, rim, own, acc, *chunks)
+    )(room, qa, rim, own, acc, *chunks)
 
 
 def shards(queries, frames_kv, summary_kv, lengths, caps):
     row = lax.axis_index("row")
-    ids = jnp.stack([row, lax.axis_index("z"), lax.axis_index("y"), lax.axis_index("x")]).astype(jnp.int32)
     slot = lax.broadcasted_iota(jnp.int32, (ZS, HALF, 4 * HD), 1) + HALF * row
     entry = lax.broadcasted_iota(jnp.int32, (ZS, HALF, 4 * HD), 2)
     mine = jnp.broadcast_to(summary_kv, (ZS, HALF, 4 * HD))
@@ -314,30 +324,28 @@
 
     own, column = lax.optimization_barrier((own, column))
     columns = [column] + [plane_shift(column, 0, d) for d in DA[1:]]
-    qa, acc = attend_local(ids, queries[0], rim, own)
+    qa, acc = attend_local(queries[0], rim, own)
     columns, qa, acc = lax.optimization_barrier((columns, qa, acc))
     near = jnp.stack(columns, axis=1)
     near = near.reshape(len(DA) * COLUMN, 4 * HD)
-    half = near.shape[0] // 2
     near_other = other_core(near)
     one = plane_shift(near, 1, 1)
     three = plane_shift(near, 1, 3)
     zero_places = ((0, 0, 0), (1, 0, 0))
-    acc = attend_remote(ids, qa, acc, (near, near_other), zero_places)
-    one, three, acc = lax.optimization_barrier((one, three, acc))
-    two_low = plane_shift(one[:half], 1, 1)
-    two_high = plane_shift(three[half:], 1, 3)
-    one_other, three_other = other_core(one), other_core(three)
-    one_places, three_places = ((0, 1, 0), (1, 1, 0)), ((0, 3, 0), (1, 3, 0))
-    acc = attend_remote(ids, qa, acc, (one, one_other), one_places)
-    two_low, two_high, acc = lax.optimization_barrier((two_low, two_high, acc))
-    low_other, high_other = other_core(two_low), other_core(two_high)
-    acc = attend_remote(ids, qa, acc, (three, three_other), three_places)
-
-    chunks = (two_low, low_other, two_high, high_other)
-    chunks += (near, near_other, one, one_other, three, three_other)
-    places = ((0, 2, 0), (1, 2, 0), (0, 2, 1), (1, 2, 1)) + zero_places + one_places + three_places
-    return attend_last(ids, lengths, qa, rim, own, acc, chunks, places, 4)[None]
+    acc = attend_remote(qa, acc, (near, near_other), zero_places)
+    one, acc = lax.optimization_barrier((one, acc))
+    two = plane_shift(one, 1, 1)
+    one_other = other_core(one)
+    three, acc = lax.optimization_barrier((three, acc))
+    three_other = other_core(three)
+    far_places = ((0, 1, 0), (1, 1, 0), (0, 3, 0), (1, 3, 0))
+    acc = attend_remote(qa, acc, (one, one_other, three, three_other), far_places)
+    two, acc = lax.optimization_barrier((two, acc))
+    two_other = other_core(two)
+
+    chunks = (two, two_other, near, near_other, one, one_other, three, three_other)
+    places = ((0, 2, 0), (1, 2, 0)) + zero_places + far_places
+    return attend_last(lengths, qa, rim, own, acc, chunks, places, 2)[None]
 
 
 def solution(mesh):

time: 61.6 us -> 57.7 us (0.937)
  Pallas kernels: 21.4 us -> 9.42 us
  waiting for transfers between devices: 8.25 us -> 18.6 us
  starting transfers between devices: 25.5 us -> 23.3 us
    pallas_call x3 -> x2, Pallas kernels: 13.3 us -> 4.46 us  [attend_remote(): pl.pallas_call(functools.partial(remote_kernel, places), out_shape=ACC, i...]
    ppermute x7 -> x6, waiting for transfers between devices: 2.5 us -> 9.64 us  [plane_shift(): return lax.ppermute(block, PLANE, route)]
    ppermute x5 -> x4, waiting for transfers between devices: 0.01 us -> 3.17 us  [other_core(): return lax.ppermute(block, 'row', [(0, 1), (1, 0)])]
    ppermute x7 -> x6, starting transfers between devices: 9.81 us -> 7.06 us  [plane_shift(): return lax.ppermute(block, PLANE, route)]
    pallas_call x1, Pallas kernels: 5.59 us -> 3.01 us  [attend_last(): pl.pallas_call(functools.partial(last_kernel, places, new), out_shape=jax...]
    ppermute x5 -> x4, starting transfers between devices: 5.6 us -> 6.23 us  [other_core(): return lax.ppermute(block, 'row', [(0, 1), (1, 0)])]
  transfers between devices with their start and end apart: 14 -> 12, of which waited for: 2 -> 6; matrix products, arithmetic and copies ran while one was open for 2% -> 2% of each run, Pallas kernels for 26% -> 11%
where the time goes in v3:
time: 57.7 us; the launch traced here: 57.4 us
  starting transfers between devices  23.3 us (40%)
  waiting for transfers between devices  18.6 us (32%)
  Pallas kernels  9.42 us (16%)
  local copies, waits for them, and re-layouts  3.05 us (5%)
  other arithmetic  1.54 us (3%)
  between operations  1.39 us (2%)
    ppermute x6, waiting for transfers between devices, plane_shift(): return lax.ppermute(block, PLANE, route)  9.64 us
    all_to_all x1, starting transfers between devices, shards(): column = lax.all_to_all(copies, 'z', 0, 0, tiled=True)  9.01 us
    ppermute x6, starting transfers between devices, plane_shift(): return lax.ppermute(block, PLANE, route)  7.06 us
    ppermute x4, starting transfers between devices, other_core(): return lax.ppermute(block, 'row', [(0, 1), (1, 0)])  6.23 us
    all_to_all x1, waiting for transfers between devices, shards(): column = lax.all_to_all(copies, 'z', 0, 0, tiled=True)  5.81 us
    pallas_call x2, Pallas kernels, attend_remote(): pl.pallas_call(functools.partial(remote_kernel, places), out_shape=ACC, i...  4.46 us
    ppermute x4, waiting for transfers between devices, other_core(): return lax.ppermute(block, 'row', [(0, 1), (1, 0)])  3.17 us
    pallas_call x1, Pallas kernels, attend_last(): pl.pallas_call(functools.partial(last_kernel, places, new), out_shape=jax...  3.01 us
  transfers between devices with their start and end apart: 12, of which 6 were waited for; matrix products, arithmetic and copies ran while one was open for 2% of the time, Pallas kernels for 11%

profile of v3, /device:TPU:1, one launch (start us, length us, event | category | flops | bytes accessed | tf_op | source)
XLA Modules:
  0.0 57.4 jit_solution(15123507598828364016)
XLA Ops:
  0.7 1.5 %and_select_fusion = bf16[8,16,512]{2,1,0:T(8,128)(2,1)} fusion(pred[512]{0:T(512)(128)(4,1)S(1)} %iota_compare_fusion, pred[16]{0:T(512)(128)(4,1)S(1)} %add_compare_fusion, bf16[16,512]{1,0:T(8,128)(2,1)} %bitcast.30), kind=kLoop, calls=%fused_computation.1 | loop fusion | flops 131072 | bytes 147984 | tf_op jit(solution)/shard_map/jit(_where)/select_n | solution.py:320
  2.1 9.0 %all-to-all-start = ((bf16[8,16,512]{2,1,0:T(8,128)(2,1)}), bf16[8,16,512]{2,1,0:T(8,128)(2,1)S(1)}, u32[]{:S(2)}, u32[]{:S(2)}) async-start(bf16[8,16,512]{2,1,0:T(8,128)(2,1)} %and_select_fusion), calls=%async_computation | async-start | bytes 262144 | tf_op jit(solution)/shard_map/all_to_all | solution.py:322
  11.1 0.9 %slice.3 = bf16[128,512]{1,0:T(8,128)(2,1)S(1)} slice(bf16[256,512]{1,0:T(8,128)(2,1)} %bitcast.22), slice={[128:256], [0:512]} | slice | bytes 262144 | tf_op jit(solution)/shard_map/slice | solution.py:323
  12.1 1.0 %collective-permute-start.3 = (bf16[128,512]{1,0:T(8,128)(2,1)S(1)}, bf16[128,512]{1,0:T(8,128)(2,1)S(1)}, u32[]{:S(2)}, u32[]{:S(2)}) collective-permute-start(bf16[128,512]{1,0:T(8,128)(2,1)S(1)} %slice.3), channel_id=1, source_target_pairs={{0,1},{1,0},{2,3},{3,2},{4,5},{5,4},{6,7},{7,6},{8,9},{9,8},{10,11... | collective-permute-start | bytes 393224 | tf_op jit(solution)/shard_map/ppermute | solution.py:323
  13.1 5.8 %all-to-all-done = bf16[8,16,512]{2,1,0:T(8,128)(2,1)S(1)} async-done(((bf16[8,16,512]{2,1,0:T(8,128)(2,1)}), bf16[8,16,512]{2,1,0:T(8,128)(2,1)S(1)}, u32[]{:S(2)}, u32[]{:S(2)}) %all-to-all-start) | async-done | bytes 131104 | tf_op jit(solution)/shard_map/all_to_all | solution.py:322
  18.9 1.3 %collective-permute-start = (bf16[8,16,512]{2,1,0:T(8,128)(2,1)S(1)}, bf16[8,16,512]{2,1,0:T(8,128)(2,1)S(1)}, u32[]{:S(2)}, u32[]{:S(2)}) collective-permute-start(bf16[8,16,512]{2,1,0:T(8,128)(2,1)S(1)} %all-to-all-done), channel_id=1, source_target_pairs={{0,2},{1,9},{2,4},{3,11},{4,6},{5,13},{6,0},{7,15},{8,10},{9,17},{... | collective-permute-start | bytes 393224 | tf_op jit(solution)/shard_map/ppermute | solution.py:46
  20.2 1.4 %collective-permute-start.1 = (bf16[8,16,512]{2,1,0:T(8,128)(2,1)S(1)}, bf16[8,16,512]{2,1,0:T(8,128)(2,1)S(1)}, u32[]{:S(2)}, u32[]{:S(2)}) collective-permute-start(bf16[8,16,512]{2,1,0:T(8,128)(2,1)S(1)} %all-to-all-done), channel_id=1, source_target_pairs={{0,6},{1,25},{2,0},{3,27},{4,2},{5,29},{6,4},{7,31},{8,14},{9,1},{... | collective-permute-start | bytes 393224 | tf_op jit(solution)/shard_map/ppermute | solution.py:46
  21.7 1.6 %collective-permute-start.2 = (bf16[8,16,512]{2,1,0:T(8,128)(2,1)S(1)}, bf16[8,16,512]{2,1,0:T(8,128)(2,1)S(1)}, u32[]{:S(2)}, u32[]{:S(2)}) collective-permute-start(bf16[8,16,512]{2,1,0:T(8,128)(2,1)S(1)} %all-to-all-done), channel_id=1, source_target_pairs={{0,4},{1,17},{2,6},{3,19},{4,0},{5,21},{6,2},{7,23},{8,12},{9,25},... | collective-permute-start | bytes 393224 | tf_op jit(solution)/shard_map/ppermute | solution.py:46
  23.3 0.0 collective-permute-done.3.rim_ref
  23.3 0.0 copy-start
  23.3 0.9 %copy-done = bf16[1,256,512]{2,1,0:T(8,128)(2,1)S(1)} copy-done((bf16[1,256,512]{2,1,0:T(8,128)(2,1)S(1)}, bf16[1,256,512]{2,1,0:T(8,128)(2,1)}, u32[]{:S(2)}) %copy-start) | copy-done | bytes 262168
  24.2 0.0 copy-start.2
  24.3 1.2 %copy-done.2 = bf16[1,256,1792]{2,1,0:T(8,128)(2,1)S(1)} copy-done((bf16[1,256,1792]{2,1,0:T(8,128)(2,1)S(1)}, bf16[1,256,1792]{2,1,0:T(8,128)(2,1)}, u32[]{:S(2)}) %copy-start.2) | copy-done | bytes 917528
  25.4 2.0 %local.1 = (bf16[2,1792,256]{2,1,0:T(8,128)(2,1)S(1)}, f32[2,1792,256]{2,1,0:T(8,128)S(1)}) custom-call(bf16[256,1792]{1,0:T(8,128)(2,1)S(1)} %bitcast.25, bf16[128,512]{1,0:T(8,128)(2,1)S(1)} %collective-permute-done.3.rim_ref, bf16[256,512]{1,0:T(8,128)(2,1)S(1)} %bitcast.23), custom_call_target="tpu_custom_call" | custom-call | flops 3758096384 | bytes 1048576 | tf_op jit(solution)/shard_map/local/pallas_call | solution.py:275
  27.4 0.0 collective-permute-done
  27.4 0.0 collective-permute-done.1
  27.4 0.0 collective-permute-done.2
  27.4 0.1 pad_maximum_fusion
  27.5 3.6 %collective-permute-start.5 = (bf16[512,512]{1,0:T(8,128)(2,1)S(1)}, bf16[512,512]{1,0:T(8,128)(2,1)S(1)}, u32[]{:S(2)}, u32[]{:S(2)}) collective-permute-start(bf16[512,512]{1,0:T(8,128)(2,1)S(1)} %bitcast.17), channel_id=1, source_target_pairs={{0,1},{1,0},{2,3},{3,2},{4,5},{5,4},{6,7},{7,6},{8,9},{9,8},{10,11... | collective-permute-start | bytes 1572872 | tf_op jit(solution)/shard_map/ppermute | solution.py:50
  31.1 0.0 collective-permute-start.4
  31.1 2.7 %collective-permute-start.7 = (bf16[512,512]{1,0:T(8,128)(2,1)S(1)}, bf16[512,512]{1,0:T(8,128)(2,1)S(1)}, u32[]{:S(2)}, u32[]{:S(2)}) collective-permute-start(bf16[512,512]{1,0:T(8,128)(2,1)S(1)} %bitcast.19), channel_id=1, source_target_pairs={{0,24},{1,7},{2,26},{3,1},{4,28},{5,3},{6,30},{7,5},{8,0},{9,15},{... | collective-permute-start | bytes 1572872 | tf_op jit(solution)/shard_map/ppermute | solution.py:46
  33.7 0.0 collective-permute-done.5.rest_1_.rest_3_
  33.7 2.1 %remote.2.acc_ref = f32[2,1792,256]{2,1,0:T(8,128)S(1)} custom-call(bf16[2,1792,256]{2,1,0:T(8,128)(2,1)S(1)} %get-tuple-element.29.qa_ref, f32[2,1792,256]{2,1,0:T(8,128)S(1)} %get-tuple-element.34.acc_ref, bf16[512,512]{1,0:T(8,128)(2,1)S(1)} %bitcast.20, bf16[512,512]{1,0:T(8,128)(2,1)S(1)} %collective-permute-done.5.rest_1_.rest_3_), custom_call_target="tpu_custom_call" | custom-call | flops 7516192768 | bytes 1048576 | tf_op jit(solution)/shard_map/remote/pallas_call | solution.py:289
  35.9 0.0 copy-start.1
  35.9 4.7 %collective-permute-done.4.rest_0_.rest_4_ = bf16[512,512]{1,0:T(8,128)(2,1)S(1)} collective-permute-done((bf16[512,512]{1,0:T(8,128)(2,1)S(1)}, bf16[512,512]{1,0:T(8,128)(2,1)S(1)}, u32[]{:S(2)}, u32[]{:S(2)}) %collective-permute-start.4) | collective-permute-done | bytes 524320 | tf_op jit(solution)/shard_map/ppermute | solution.py:46
  40.6 0.0 collective-permute-done.7.rest_2_.rest_6_
  40.6 1.3 %collective-permute-start.9 = (bf16[512,512]{1,0:T(8,128)(2,1)S(1)}, bf16[512,512]{1,0:T(8,128)(2,1)S(1)}, u32[]{:S(2)}, u32[]{:S(2)}) collective-permute-start(bf16[512,512]{1,0:T(8,128)(2,1)S(1)} %collective-permute-done.7.rest_2_.rest_6_), channel_id=1, source_target_pairs={{0,1},{1,0},{2,3},{3,2},{4,5},{5,4},{6,7},{7,6},{8,9},{9,8},{10,11... | collective-permute-start | bytes 1572872 | tf_op jit(solution)/shard_map/ppermute | solution.py:50
  41.9 0.0 collective-permute-start.8
  41.9 0.0 collective-permute-start.6
  41.9 1.5 %collective-permute-done.9.rest_3_.rest_7_ = bf16[512,512]{1,0:T(8,128)(2,1)S(1)} collective-permute-done((bf16[512,512]{1,0:T(8,128)(2,1)S(1)}, bf16[512,512]{1,0:T(8,128)(2,1)S(1)}, u32[]{:S(2)}, u32[]{:S(2)}) %collective-permute-start.9) | collective-permute-done | bytes 524320 | tf_op jit(solution)/shard_map/ppermute | solution.py:50
  43.4 0.7 %collective-permute-done.8.rest_1_.rest_5_ = bf16[512,512]{1,0:T(8,128)(2,1)S(1)} collective-permute-done((bf16[512,512]{1,0:T(8,128)(2,1)S(1)}, bf16[512,512]{1,0:T(8,128)(2,1)S(1)}, u32[]{:S(2)}, u32[]{:S(2)}) %collective-permute-start.8) | collective-permute-done | bytes 524320 | tf_op jit(solution)/shard_map/ppermute | solution.py:50
  44.2 2.4 %remote.3.acc_ref = f32[2,1792,256]{2,1,0:T(8,128)S(1)} custom-call(bf16[2,1792,256]{2,1,0:T(8,128)(2,1)S(1)} %get-tuple-element.29.qa_ref, f32[2,1792,256]{2,1,0:T(8,128)S(1)} %remote.2.acc_ref, bf16[512,512]{1,0:T(8,128)(2,1)S(1)} %collective-permute-done.4.rest_0_.rest_4_, bf16[512,512]{1,0:T(8,128)(2,1)S(1)} %collective-permute-done.8.rest_1_.rest_5_, ...), custom_call_target="tpu_custom_call" | custom-call | flops 15032385536 | bytes 1048576 | tf_op jit(solution)/shard_map/remote/pallas_call | solution.py:289
  46.6 4.9 %collective-permute-done.6.rest_0_ = bf16[512,512]{1,0:T(8,128)(2,1)S(1)} collective-permute-done((bf16[512,512]{1,0:T(8,128)(2,1)S(1)}, bf16[512,512]{1,0:T(8,128)(2,1)S(1)}, u32[]{:S(2)}, u32[]{:S(2)}) %collective-permute-start.6) | collective-permute-done | bytes 524320 | tf_op jit(solution)/shard_map/ppermute | solution.py:46
  51.5 1.4 %collective-permute-start.10 = (bf16[512,512]{1,0:T(8,128)(2,1)S(1)}, bf16[512,512]{1,0:T(8,128)(2,1)S(1)}, u32[]{:S(2)}, u32[]{:S(2)}) collective-permute-start(bf16[512,512]{1,0:T(8,128)(2,1)S(1)} %collective-permute-done.6.rest_0_), channel_id=1, source_target_pairs={{0,1},{1,0},{2,3},{3,2},{4,5},{5,4},{6,7},{7,6},{8,9},{9,8},{10,11... | collective-permute-start | bytes 1572872 | tf_op jit(solution)/shard_map/ppermute | solution.py:50
  53.5 0.9 %collective-permute-done.10.rest_1_ = bf16[512,512]{1,0:T(8,128)(2,1)S(1)} collective-permute-done((bf16[512,512]{1,0:T(8,128)(2,1)S(1)}, bf16[512,512]{1,0:T(8,128)(2,1)S(1)}, u32[]{:S(2)}, u32[]{:S(2)}) %collective-permute-start.10) | collective-permute-done | bytes 524320 | tf_op jit(solution)/shard_map/ppermute | solution.py:50
  54.4 0.0 copy-done.1
  54.4 3.0 %last.1 = bf16[256,1792]{1,0:T(8,128)(2,1)} custom-call(s32[1]{0:T(128)S(6)} %copy.9.room_ref, bf16[2,1792,256]{2,1,0:T(8,128)(2,1)S(1)} %get-tuple-element.29.qa_ref, bf16[128,512]{1,0:T(8,128)(2,1)S(1)} %collective-permute-done.3.rim_ref, bf16[256,512]{1,0:T(8,128)(2,1)S(1)} %bitcast.24, f32[2,1792,256]{2,1,0:T(8,128)S(1)} %remote.3.acc_ref, ...), custom_call_target="tpu_custom_call" | custom-call | flops 30064771072 | bytes 1048576 | tf_op jit(solution)/shard_map/last/pallas_call | solution.py:303
  (2 shorter events, 0.0 us)
Async XLA Ops:
  2.1 16.8 %all-to-all-start = ((bf16[8,16,512]{2,1,0:T(8,128)(2,1)}), bf16[8,16,512]{2,1,0:T(8,128)(2,1)S(1)}, u32[]{:S(2)}, u32[]{:S(2)}) async-start(bf16[8,16,512]{2,1,0:T(8,128)(2,1)} %and_select_fusion), calls=%async_computation | async-start | bytes 262144 | tf_op jit(solution)/shard_map/all_to_all | solution.py:322
  12.1 11.2 %collective-permute-start.3 = (bf16[128,512]{1,0:T(8,128)(2,1)S(1)}, bf16[128,512]{1,0:T(8,128)(2,1)S(1)}, u32[]{:S(2)}, u32[]{:S(2)}) collective-permute-start(bf16[128,512]{1,0:T(8,128)(2,1)S(1)} %slice.3), channel_id=1, source_target_pairs={{0,1},{1,0},{2,3},{3,2},{4,5},{5,4},{6,7},{7,6},{8,9},{9,8},{10,11... | collective-permute-start | bytes 393224 | tf_op jit(solution)/shard_map/ppermute | solution.py:323
  18.9 8.5 %collective-permute-start = (bf16[8,16,512]{2,1,0:T(8,128)(2,1)S(1)}, bf16[8,16,512]{2,1,0:T(8,128)(2,1)S(1)}, u32[]{:S(2)}, u32[]{:S(2)}) collective-permute-start(bf16[8,16,512]{2,1,0:T(8,128)(2,1)S(1)} %all-to-all-done), channel_id=1, source_target_pairs={{0,2},{1,9},{2,4},{3,11},{4,6},{5,13},{6,0},{7,15},{8,10},{9,17},{... | collective-permute-start | bytes 393224 | tf_op jit(solution)/shard_map/ppermute | solution.py:46
  20.2 7.2 %collective-permute-start.1 = (bf16[8,16,512]{2,1,0:T(8,128)(2,1)S(1)}, bf16[8,16,512]{2,1,0:T(8,128)(2,1)S(1)}, u32[]{:S(2)}, u32[]{:S(2)}) collective-permute-start(bf16[8,16,512]{2,1,0:T(8,128)(2,1)S(1)} %all-to-all-done), channel_id=1, source_target_pairs={{0,6},{1,25},{2,0},{3,27},{4,2},{5,29},{6,4},{7,31},{8,14},{9,1},{... | collective-permute-start | bytes 393224 | tf_op jit(solution)/shard_map/ppermute | solution.py:46
  21.7 5.8 %collective-permute-start.2 = (bf16[8,16,512]{2,1,0:T(8,128)(2,1)S(1)}, bf16[8,16,512]{2,1,0:T(8,128)(2,1)S(1)}, u32[]{:S(2)}, u32[]{:S(2)}) collective-permute-start(bf16[8,16,512]{2,1,0:T(8,128)(2,1)S(1)} %all-to-all-done), channel_id=1, source_target_pairs={{0,4},{1,17},{2,6},{3,19},{4,0},{5,21},{6,2},{7,23},{8,12},{9,25},... | collective-permute-start | bytes 393224 | tf_op jit(solution)/shard_map/ppermute | solution.py:46
  23.3 1.0 %copy-start = (bf16[1,256,512]{2,1,0:T(8,128)(2,1)S(1)}, bf16[1,256,512]{2,1,0:T(8,128)(2,1)}, u32[]{:S(2)}) copy-start(bf16[1,256,512]{2,1,0:T(8,128)(2,1)} %param.6) | copy-start | bytes 786436
  24.2 1.2 %copy-start.2 = (bf16[1,256,1792]{2,1,0:T(8,128)(2,1)S(1)}, bf16[1,256,1792]{2,1,0:T(8,128)(2,1)}, u32[]{:S(2)}) copy-start(bf16[1,256,1792]{2,1,0:T(8,128)(2,1)} %param.5) | copy-start | bytes 2752516
  27.5 6.2 %collective-permute-start.5 = (bf16[512,512]{1,0:T(8,128)(2,1)S(1)}, bf16[512,512]{1,0:T(8,128)(2,1)S(1)}, u32[]{:S(2)}, u32[]{:S(2)}) collective-permute-start(bf16[512,512]{1,0:T(8,128)(2,1)S(1)} %bitcast.17), channel_id=1, source_target_pairs={{0,1},{1,0},{2,3},{3,2},{4,5},{5,4},{6,7},{7,6},{8,9},{9,8},{10,11... | collective-permute-start | bytes 1572872 | tf_op jit(solution)/shard_map/ppermute | solution.py:50
  31.1 9.5 %collective-permute-start.4 = (bf16[512,512]{1,0:T(8,128)(2,1)S(1)}, bf16[512,512]{1,0:T(8,128)(2,1)S(1)}, u32[]{:S(2)}, u32[]{:S(2)}) collective-permute-start(bf16[512,512]{1,0:T(8,128)(2,1)S(1)} %bitcast.18), channel_id=1, source_target_pairs={{0,8},{1,3},{2,10},{3,5},{4,12},{5,7},{6,14},{7,1},{8,16},{9,11},{... | collective-permute-start | bytes 1572872 | tf_op jit(solution)/shard_map/ppermute | solution.py:46
  31.1 9.5 %collective-permute-start.7 = (bf16[512,512]{1,0:T(8,128)(2,1)S(1)}, bf16[512,512]{1,0:T(8,128)(2,1)S(1)}, u32[]{:S(2)}, u32[]{:S(2)}) collective-permute-start(bf16[512,512]{1,0:T(8,128)(2,1)S(1)} %bitcast.19), channel_id=1, source_target_pairs={{0,24},{1,7},{2,26},{3,1},{4,28},{5,3},{6,30},{7,5},{8,0},{9,15},{... | collective-permute-start | bytes 1572872 | tf_op jit(solution)/shard_map/ppermute | solution.py:46
  35.9 18.5 %copy-start.1 = (bf16[1,256,512]{2,1,0:T(8,128)(2,1)S(1)}, bf16[1,256,512]{2,1,0:T(8,128)(2,1)}, u32[]{:S(2)}) copy-start(bf16[1,256,512]{2,1,0:T(8,128)(2,1)} %param.6) | copy-start | bytes 786436
  40.6 2.8 %collective-permute-start.9 = (bf16[512,512]{1,0:T(8,128)(2,1)S(1)}, bf16[512,512]{1,0:T(8,128)(2,1)S(1)}, u32[]{:S(2)}, u32[]{:S(2)}) collective-permute-start(bf16[512,512]{1,0:T(8,128)(2,1)S(1)} %collective-permute-done.7.rest_2_.rest_6_), channel_id=1, source_target_pairs={{0,1},{1,0},{2,3},{3,2},{4,5},{5,4},{6,7},{7,6},{8,9},{9,8},{10,11... | collective-permute-start | bytes 1572872 | tf_op jit(solution)/shard_map/ppermute | solution.py:50
  41.9 2.3 %collective-permute-start.8 = (bf16[512,512]{1,0:T(8,128)(2,1)S(1)}, bf16[512,512]{1,0:T(8,128)(2,1)S(1)}, u32[]{:S(2)}, u32[]{:S(2)}) collective-permute-start(bf16[512,512]{1,0:T(8,128)(2,1)S(1)} %collective-permute-done.4.rest_0_.rest_4_), channel_id=1, source_target_pairs={{0,1},{1,0},{2,3},{3,2},{4,5},{5,4},{6,7},{7,6},{8,9},{9,8},{10,11... | collective-permute-start | bytes 1572872 | tf_op jit(solution)/shard_map/ppermute | solution.py:50
  41.9 9.5 %collective-permute-start.6 = (bf16[512,512]{1,0:T(8,128)(2,1)S(1)}, bf16[512,512]{1,0:T(8,128)(2,1)S(1)}, u32[]{:S(2)}, u32[]{:S(2)}) collective-permute-start(bf16[512,512]{1,0:T(8,128)(2,1)S(1)} %collective-permute-done.4.rest_0_.rest_4_), channel_id=1, source_target_pairs={{0,8},{1,3},{2,10},{3,5},{4,12},{5,7},{6,14},{7,1},{8,16},{9,11},{... | collective-permute-start | bytes 1572872 | tf_op jit(solution)/shard_map/ppermute | solution.py:46
  51.5 2.9 %collective-permute-start.10 = (bf16[512,512]{1,0:T(8,128)(2,1)S(1)}, bf16[512,512]{1,0:T(8,128)(2,1)S(1)}, u32[]{:S(2)}, u32[]{:S(2)}) collective-permute-start(bf16[512,512]{1,0:T(8,128)(2,1)S(1)} %collective-permute-done.6.rest_0_), channel_id=1, source_target_pairs={{0,1},{1,0},{2,3},{3,2},{4,5},{5,4},{6,7},{7,6},{8,9},{9,8},{10,11... | collective-permute-start | bytes 1572872 | tf_op jit(solution)/shard_map/ppermute | solution.py:50

commit v4 on v3

--- a/solution.py
+++ b/solution.py
@@ -323,7 +323,8 @@
     rim = lax.ppermute(own[TOKENS - WINDOW :], "row", [(0, 1), (1, 0)])
 
     own, column = lax.optimization_barrier((own, column))
-    columns = [column] + [plane_shift(column, 0, d) for d in DA[1:]]
+    opposite = plane_shift(column, 0, 2)
+    columns = [column] + [plane_shift(column, 0, d) for d in DA[1:3]] + [opposite]
     qa, acc = attend_local(queries[0], rim, own)
     columns, qa, acc = lax.optimization_barrier((columns, qa, acc))
     near = jnp.stack(columns, axis=1)

time: 57.7 us -> 57.7 us (level)
  no operation moved by 1% of the time
where the time goes in v4:
time: 57.7 us; the launch traced here: 57.4 us
  starting transfers between devices  23.3 us (40%)
  waiting for transfers between devices  18.6 us (32%)
  Pallas kernels  9.42 us (16%)
  local copies, waits for them, and re-layouts  3.05 us (5%)
  other arithmetic  1.54 us (3%)
  between operations  1.39 us (2%)
    ppermute x6, waiting for transfers between devices, plane_shift(): return lax.ppermute(block, PLANE, route)  9.64 us
    all_to_all x1, starting transfers between devices, shards(): column = lax.all_to_all(copies, 'z', 0, 0, tiled=True)  9.01 us
    ppermute x6, starting transfers between devices, plane_shift(): return lax.ppermute(block, PLANE, route)  7.06 us
    ppermute x4, starting transfers between devices, other_core(): return lax.ppermute(block, 'row', [(0, 1), (1, 0)])  6.23 us
    all_to_all x1, waiting for transfers between devices, shards(): column = lax.all_to_all(copies, 'z', 0, 0, tiled=True)  5.81 us
    pallas_call x2, Pallas kernels, attend_remote(): pl.pallas_call(functools.partial(remote_kernel, places), out_shape=ACC, i...  4.46 us
    ppermute x4, waiting for transfers between devices, other_core(): return lax.ppermute(block, 'row', [(0, 1), (1, 0)])  3.17 us
    pallas_call x1, Pallas kernels, attend_last(): pl.pallas_call(functools.partial(last_kernel, places, new), out_shape=jax...  3.01 us
  transfers between devices with their start and end apart: 12, of which 6 were waited for; matrix products, arithmetic and copies ran while one was open for 2% of the time, Pallas kernels for 11%

profile of v4, /device:TPU:1, one launch (start us, length us, event | category | flops | bytes accessed | tf_op | source)
XLA Modules:
  0.0 57.4 jit_solution(15123507598828364016)
XLA Ops:
  0.7 1.5 %and_select_fusion = bf16[8,16,512]{2,1,0:T(8,128)(2,1)} fusion(pred[512]{0:T(512)(128)(4,1)S(1)} %iota_compare_fusion, pred[16]{0:T(512)(128)(4,1)S(1)} %add_compare_fusion, bf16[16,512]{1,0:T(8,128)(2,1)} %bitcast.30), kind=kLoop, calls=%fused_computation.1 | loop fusion | flops 131072 | bytes 147984 | tf_op jit(solution)/shard_map/jit(_where)/select_n | solution.py:320
  2.1 9.0 %all-to-all-start = ((bf16[8,16,512]{2,1,0:T(8,128)(2,1)}), bf16[8,16,512]{2,1,0:T(8,128)(2,1)S(1)}, u32[]{:S(2)}, u32[]{:S(2)}) async-start(bf16[8,16,512]{2,1,0:T(8,128)(2,1)} %and_select_fusion), calls=%async_computation | async-start | bytes 262144 | tf_op jit(solution)/shard_map/all_to_all | solution.py:322
  11.1 0.9 %slice.3 = bf16[128,512]{1,0:T(8,128)(2,1)S(1)} slice(bf16[256,512]{1,0:T(8,128)(2,1)} %bitcast.22), slice={[128:256], [0:512]} | slice | bytes 262144 | tf_op jit(solution)/shard_map/slice | solution.py:323
  12.1 1.0 %collective-permute-start.3 = (bf16[128,512]{1,0:T(8,128)(2,1)S(1)}, bf16[128,512]{1,0:T(8,128)(2,1)S(1)}, u32[]{:S(2)}, u32[]{:S(2)}) collective-permute-start(bf16[128,512]{1,0:T(8,128)(2,1)S(1)} %slice.3), channel_id=1, source_target_pairs={{0,1},{1,0},{2,3},{3,2},{4,5},{5,4},{6,7},{7,6},{8,9},{9,8},{10,11... | collective-permute-start | bytes 393224 | tf_op jit(solution)/shard_map/ppermute | solution.py:323
  13.1 5.8 %all-to-all-done = bf16[8,16,512]{2,1,0:T(8,128)(2,1)S(1)} async-done(((bf16[8,16,512]{2,1,0:T(8,128)(2,1)}), bf16[8,16,512]{2,1,0:T(8,128)(2,1)S(1)}, u32[]{:S(2)}, u32[]{:S(2)}) %all-to-all-start) | async-done | bytes 131104 | tf_op jit(solution)/shard_map/all_to_all | solution.py:322
  18.9 1.3 %collective-permute-start = (bf16[8,16,512]{2,1,0:T(8,128)(2,1)S(1)}, bf16[8,16,512]{2,1,0:T(8,128)(2,1)S(1)}, u32[]{:S(2)}, u32[]{:S(2)}) collective-permute-start(bf16[8,16,512]{2,1,0:T(8,128)(2,1)S(1)} %all-to-all-done), channel_id=1, source_target_pairs={{0,2},{1,9},{2,4},{3,11},{4,6},{5,13},{6,0},{7,15},{8,10},{9,17},{... | collective-permute-start | bytes 393224 | tf_op jit(solution)/shard_map/ppermute | solution.py:46
  20.2 1.4 %collective-permute-start.1 = (bf16[8,16,512]{2,1,0:T(8,128)(2,1)S(1)}, bf16[8,16,512]{2,1,0:T(8,128)(2,1)S(1)}, u32[]{:S(2)}, u32[]{:S(2)}) collective-permute-start(bf16[8,16,512]{2,1,0:T(8,128)(2,1)S(1)} %all-to-all-done), channel_id=1, source_target_pairs={{0,6},{1,25},{2,0},{3,27},{4,2},{5,29},{6,4},{7,31},{8,14},{9,1},{... | collective-permute-start | bytes 393224 | tf_op jit(solution)/shard_map/ppermute | solution.py:46
  21.7 1.6 %collective-permute-start.2 = (bf16[8,16,512]{2,1,0:T(8,128)(2,1)S(1)}, bf16[8,16,512]{2,1,0:T(8,128)(2,1)S(1)}, u32[]{:S(2)}, u32[]{:S(2)}) collective-permute-start(bf16[8,16,512]{2,1,0:T(8,128)(2,1)S(1)} %all-to-all-done), channel_id=1, source_target_pairs={{0,4},{1,17},{2,6},{3,19},{4,0},{5,21},{6,2},{7,23},{8,12},{9,25},... | collective-permute-start | bytes 393224 | tf_op jit(solution)/shard_map/ppermute | solution.py:46
  23.3 0.0 collective-permute-done.3.rim_ref
  23.3 0.0 copy-start
  23.3 0.9 %copy-done = bf16[1,256,512]{2,1,0:T(8,128)(2,1)S(1)} copy-done((bf16[1,256,512]{2,1,0:T(8,128)(2,1)S(1)}, bf16[1,256,512]{2,1,0:T(8,128)(2,1)}, u32[]{:S(2)}) %copy-start) | copy-done | bytes 262168
  24.2 0.0 copy-start.2
  24.3 1.2 %copy-done.2 = bf16[1,256,1792]{2,1,0:T(8,128)(2,1)S(1)} copy-done((bf16[1,256,1792]{2,1,0:T(8,128)(2,1)S(1)}, bf16[1,256,1792]{2,1,0:T(8,128)(2,1)}, u32[]{:S(2)}) %copy-start.2) | copy-done | bytes 917528
  25.4 2.0 %local.1 = (bf16[2,1792,256]{2,1,0:T(8,128)(2,1)S(1)}, f32[2,1792,256]{2,1,0:T(8,128)S(1)}) custom-call(bf16[256,1792]{1,0:T(8,128)(2,1)S(1)} %bitcast.25, bf16[128,512]{1,0:T(8,128)(2,1)S(1)} %collective-permute-done.3.rim_ref, bf16[256,512]{1,0:T(8,128)(2,1)S(1)} %bitcast.23), custom_call_target="tpu_custom_call" | custom-call | flops 3758096384 | bytes 1048576 | tf_op jit(solution)/shard_map/local/pallas_call | solution.py:275
  27.4 0.0 collective-permute-done
  27.4 0.0 collective-permute-done.1
  27.4 0.0 collective-permute-done.2
  27.4 0.1 pad_maximum_fusion
  27.5 3.6 %collective-permute-start.5 = (bf16[512,512]{1,0:T(8,128)(2,1)S(1)}, bf16[512,512]{1,0:T(8,128)(2,1)S(1)}, u32[]{:S(2)}, u32[]{:S(2)}) collective-permute-start(bf16[512,512]{1,0:T(8,128)(2,1)S(1)} %bitcast.17), channel_id=1, source_target_pairs={{0,1},{1,0},{2,3},{3,2},{4,5},{5,4},{6,7},{7,6},{8,9},{9,8},{10,11... | collective-permute-start | bytes 1572872 | tf_op jit(solution)/shard_map/ppermute | solution.py:50
  31.1 0.0 collective-permute-start.4
  31.1 2.7 %collective-permute-start.7 = (bf16[512,512]{1,0:T(8,128)(2,1)S(1)}, bf16[512,512]{1,0:T(8,128)(2,1)S(1)}, u32[]{:S(2)}, u32[]{:S(2)}) collective-permute-start(bf16[512,512]{1,0:T(8,128)(2,1)S(1)} %bitcast.19), channel_id=1, source_target_pairs={{0,24},{1,7},{2,26},{3,1},{4,28},{5,3},{6,30},{7,5},{8,0},{9,15},{... | collective-permute-start | bytes 1572872 | tf_op jit(solution)/shard_map/ppermute | solution.py:46
  33.7 0.0 collective-permute-done.5.rest_1_.rest_3_
  33.7 2.1 %remote.2.acc_ref = f32[2,1792,256]{2,1,0:T(8,128)S(1)} custom-call(bf16[2,1792,256]{2,1,0:T(8,128)(2,1)S(1)} %get-tuple-element.29.qa_ref, f32[2,1792,256]{2,1,0:T(8,128)S(1)} %get-tuple-element.34.acc_ref, bf16[512,512]{1,0:T(8,128)(2,1)S(1)} %bitcast.20, bf16[512,512]{1,0:T(8,128)(2,1)S(1)} %collective-permute-done.5.rest_1_.rest_3_), custom_call_target="tpu_custom_call" | custom-call | flops 7516192768 | bytes 1048576 | tf_op jit(solution)/shard_map/remote/pallas_call | solution.py:289
  35.9 0.0 copy-start.1
  35.9 4.7 %collective-permute-done.4.rest_0_.rest_4_ = bf16[512,512]{1,0:T(8,128)(2,1)S(1)} collective-permute-done((bf16[512,512]{1,0:T(8,128)(2,1)S(1)}, bf16[512,512]{1,0:T(8,128)(2,1)S(1)}, u32[]{:S(2)}, u32[]{:S(2)}) %collective-permute-start.4) | collective-permute-done | bytes 524320 | tf_op jit(solution)/shard_map/ppermute | solution.py:46
  40.6 0.0 collective-permute-done.7.rest_2_.rest_6_
  40.6 1.3 %collective-permute-start.9 = (bf16[512,512]{1,0:T(8,128)(2,1)S(1)}, bf16[512,512]{1,0:T(8,128)(2,1)S(1)}, u32[]{:S(2)}, u32[]{:S(2)}) collective-permute-start(bf16[512,512]{1,0:T(8,128)(2,1)S(1)} %collective-permute-done.7.rest_2_.rest_6_), channel_id=1, source_target_pairs={{0,1},{1,0},{2,3},{3,2},{4,5},{5,4},{6,7},{7,6},{8,9},{9,8},{10,11... | collective-permute-start | bytes 1572872 | tf_op jit(solution)/shard_map/ppermute | solution.py:50
  41.9 0.0 collective-permute-start.8
  41.9 0.0 collective-permute-start.6
  41.9 1.5 %collective-permute-done.9.rest_3_.rest_7_ = bf16[512,512]{1,0:T(8,128)(2,1)S(1)} collective-permute-done((bf16[512,512]{1,0:T(8,128)(2,1)S(1)}, bf16[512,512]{1,0:T(8,128)(2,1)S(1)}, u32[]{:S(2)}, u32[]{:S(2)}) %collective-permute-start.9) | collective-permute-done | bytes 524320 | tf_op jit(solution)/shard_map/ppermute | solution.py:50
  43.4 0.7 %collective-permute-done.8.rest_1_.rest_5_ = bf16[512,512]{1,0:T(8,128)(2,1)S(1)} collective-permute-done((bf16[512,512]{1,0:T(8,128)(2,1)S(1)}, bf16[512,512]{1,0:T(8,128)(2,1)S(1)}, u32[]{:S(2)}, u32[]{:S(2)}) %collective-permute-start.8) | collective-permute-done | bytes 524320 | tf_op jit(solution)/shard_map/ppermute | solution.py:50
  44.2 2.4 %remote.3.acc_ref = f32[2,1792,256]{2,1,0:T(8,128)S(1)} custom-call(bf16[2,1792,256]{2,1,0:T(8,128)(2,1)S(1)} %get-tuple-element.29.qa_ref, f32[2,1792,256]{2,1,0:T(8,128)S(1)} %remote.2.acc_ref, bf16[512,512]{1,0:T(8,128)(2,1)S(1)} %collective-permute-done.4.rest_0_.rest_4_, bf16[512,512]{1,0:T(8,128)(2,1)S(1)} %collective-permute-done.8.rest_1_.rest_5_, ...), custom_call_target="tpu_custom_call" | custom-call | flops 15032385536 | bytes 1048576 | tf_op jit(solution)/shard_map/remote/pallas_call | solution.py:289
  46.6 4.9 %collective-permute-done.6.rest_0_ = bf16[512,512]{1,0:T(8,128)(2,1)S(1)} collective-permute-done((bf16[512,512]{1,0:T(8,128)(2,1)S(1)}, bf16[512,512]{1,0:T(8,128)(2,1)S(1)}, u32[]{:S(2)}, u32[]{:S(2)}) %collective-permute-start.6) | collective-permute-done | bytes 524320 | tf_op jit(solution)/shard_map/ppermute | solution.py:46
  51.5 1.4 %collective-permute-start.10 = (bf16[512,512]{1,0:T(8,128)(2,1)S(1)}, bf16[512,512]{1,0:T(8,128)(2,1)S(1)}, u32[]{:S(2)}, u32[]{:S(2)}) collective-permute-start(bf16[512,512]{1,0:T(8,128)(2,1)S(1)} %collective-permute-done.6.rest_0_), channel_id=1, source_target_pairs={{0,1},{1,0},{2,3},{3,2},{4,5},{5,4},{6,7},{7,6},{8,9},{9,8},{10,11... | collective-permute-start | bytes 1572872 | tf_op jit(solution)/shard_map/ppermute | solution.py:50
  53.5 0.9 %collective-permute-done.10.rest_1_ = bf16[512,512]{1,0:T(8,128)(2,1)S(1)} collective-permute-done((bf16[512,512]{1,0:T(8,128)(2,1)S(1)}, bf16[512,512]{1,0:T(8,128)(2,1)S(1)}, u32[]{:S(2)}, u32[]{:S(2)}) %collective-permute-start.10) | collective-permute-done | bytes 524320 | tf_op jit(solution)/shard_map/ppermute | solution.py:50
  54.4 0.0 copy-done.1
  54.4 3.0 %last.1 = bf16[256,1792]{1,0:T(8,128)(2,1)} custom-call(s32[1]{0:T(128)S(6)} %copy.9.room_ref, bf16[2,1792,256]{2,1,0:T(8,128)(2,1)S(1)} %get-tuple-element.29.qa_ref, bf16[128,512]{1,0:T(8,128)(2,1)S(1)} %collective-permute-done.3.rim_ref, bf16[256,512]{1,0:T(8,128)(2,1)S(1)} %bitcast.24, f32[2,1792,256]{2,1,0:T(8,128)S(1)} %remote.3.acc_ref, ...), custom_call_target="tpu_custom_call" | custom-call | flops 30064771072 | bytes 1048576 | tf_op jit(solution)/shard_map/last/pallas_call | solution.py:303
  (2 shorter events, 0.0 us)
Async XLA Ops:
  2.1 16.8 %all-to-all-start = ((bf16[8,16,512]{2,1,0:T(8,128)(2,1)}), bf16[8,16,512]{2,1,0:T(8,128)(2,1)S(1)}, u32[]{:S(2)}, u32[]{:S(2)}) async-start(bf16[8,16,512]{2,1,0:T(8,128)(2,1)} %and_select_fusion), calls=%async_computation | async-start | bytes 262144 | tf_op jit(solution)/shard_map/all_to_all | solution.py:322
  12.1 11.2 %collective-permute-start.3 = (bf16[128,512]{1,0:T(8,128)(2,1)S(1)}, bf16[128,512]{1,0:T(8,128)(2,1)S(1)}, u32[]{:S(2)}, u32[]{:S(2)}) collective-permute-start(bf16[128,512]{1,0:T(8,128)(2,1)S(1)} %slice.3), channel_id=1, source_target_pairs={{0,1},{1,0},{2,3},{3,2},{4,5},{5,4},{6,7},{7,6},{8,9},{9,8},{10,11... | collective-permute-start | bytes 393224 | tf_op jit(solution)/shard_map/ppermute | solution.py:323
  18.9 8.5 %collective-permute-start = (bf16[8,16,512]{2,1,0:T(8,128)(2,1)S(1)}, bf16[8,16,512]{2,1,0:T(8,128)(2,1)S(1)}, u32[]{:S(2)}, u32[]{:S(2)}) collective-permute-start(bf16[8,16,512]{2,1,0:T(8,128)(2,1)S(1)} %all-to-all-done), channel_id=1, source_target_pairs={{0,2},{1,9},{2,4},{3,11},{4,6},{5,13},{6,0},{7,15},{8,10},{9,17},{... | collective-permute-start | bytes 393224 | tf_op jit(solution)/shard_map/ppermute | solution.py:46
  20.2 7.2 %collective-permute-start.1 = (bf16[8,16,512]{2,1,0:T(8,128)(2,1)S(1)}, bf16[8,16,512]{2,1,0:T(8,128)(2,1)S(1)}, u32[]{:S(2)}, u32[]{:S(2)}) collective-permute-start(bf16[8,16,512]{2,1,0:T(8,128)(2,1)S(1)} %all-to-all-done), channel_id=1, source_target_pairs={{0,6},{1,25},{2,0},{3,27},{4,2},{5,29},{6,4},{7,31},{8,14},{9,1},{... | collective-permute-start | bytes 393224 | tf_op jit(solution)/shard_map/ppermute | solution.py:46
  21.7 5.8 %collective-permute-start.2 = (bf16[8,16,512]{2,1,0:T(8,128)(2,1)S(1)}, bf16[8,16,512]{2,1,0:T(8,128)(2,1)S(1)}, u32[]{:S(2)}, u32[]{:S(2)}) collective-permute-start(bf16[8,16,512]{2,1,0:T(8,128)(2,1)S(1)} %all-to-all-done), channel_id=1, source_target_pairs={{0,4},{1,17},{2,6},{3,19},{4,0},{5,21},{6,2},{7,23},{8,12},{9,25},... | collective-permute-start | bytes 393224 | tf_op jit(solution)/shard_map/ppermute | solution.py:46
  23.3 1.0 %copy-start = (bf16[1,256,512]{2,1,0:T(8,128)(2,1)S(1)}, bf16[1,256,512]{2,1,0:T(8,128)(2,1)}, u32[]{:S(2)}) copy-start(bf16[1,256,512]{2,1,0:T(8,128)(2,1)} %param.6) | copy-start | bytes 786436
  24.2 1.2 %copy-start.2 = (bf16[1,256,1792]{2,1,0:T(8,128)(2,1)S(1)}, bf16[1,256,1792]{2,1,0:T(8,128)(2,1)}, u32[]{:S(2)}) copy-start(bf16[1,256,1792]{2,1,0:T(8,128)(2,1)} %param.5) | copy-start | bytes 2752516
  27.5 6.2 %collective-permute-start.5 = (bf16[512,512]{1,0:T(8,128)(2,1)S(1)}, bf16[512,512]{1,0:T(8,128)(2,1)S(1)}, u32[]{:S(2)}, u32[]{:S(2)}) collective-permute-start(bf16[512,512]{1,0:T(8,128)(2,1)S(1)} %bitcast.17), channel_id=1, source_target_pairs={{0,1},{1,0},{2,3},{3,2},{4,5},{5,4},{6,7},{7,6},{8,9},{9,8},{10,11... | collective-permute-start | bytes 1572872 | tf_op jit(solution)/shard_map/ppermute | solution.py:50
  31.1 9.5 %collective-permute-start.4 = (bf16[512,512]{1,0:T(8,128)(2,1)S(1)}, bf16[512,512]{1,0:T(8,128)(2,1)S(1)}, u32[]{:S(2)}, u32[]{:S(2)}) collective-permute-start(bf16[512,512]{1,0:T(8,128)(2,1)S(1)} %bitcast.18), channel_id=1, source_target_pairs={{0,8},{1,3},{2,10},{3,5},{4,12},{5,7},{6,14},{7,1},{8,16},{9,11},{... | collective-permute-start | bytes 1572872 | tf_op jit(solution)/shard_map/ppermute | solution.py:46
  31.1 9.5 %collective-permute-start.7 = (bf16[512,512]{1,0:T(8,128)(2,1)S(1)}, bf16[512,512]{1,0:T(8,128)(2,1)S(1)}, u32[]{:S(2)}, u32[]{:S(2)}) collective-permute-start(bf16[512,512]{1,0:T(8,128)(2,1)S(1)} %bitcast.19), channel_id=1, source_target_pairs={{0,24},{1,7},{2,26},{3,1},{4,28},{5,3},{6,30},{7,5},{8,0},{9,15},{... | collective-permute-start | bytes 1572872 | tf_op jit(solution)/shard_map/ppermute | solution.py:46
  35.9 18.5 %copy-start.1 = (bf16[1,256,512]{2,1,0:T(8,128)(2,1)S(1)}, bf16[1,256,512]{2,1,0:T(8,128)(2,1)}, u32[]{:S(2)}) copy-start(bf16[1,256,512]{2,1,0:T(8,128)(2,1)} %param.6) | copy-start | bytes 786436
  40.6 2.8 %collective-permute-start.9 = (bf16[512,512]{1,0:T(8,128)(2,1)S(1)}, bf16[512,512]{1,0:T(8,128)(2,1)S(1)}, u32[]{:S(2)}, u32[]{:S(2)}) collective-permute-start(bf16[512,512]{1,0:T(8,128)(2,1)S(1)} %collective-permute-done.7.rest_2_.rest_6_), channel_id=1, source_target_pairs={{0,1},{1,0},{2,3},{3,2},{4,5},{5,4},{6,7},{7,6},{8,9},{9,8},{10,11... | collective-permute-start | bytes 1572872 | tf_op jit(solution)/shard_map/ppermute | solution.py:50
  41.9 2.3 %collective-permute-start.8 = (bf16[512,512]{1,0:T(8,128)(2,1)S(1)}, bf16[512,512]{1,0:T(8,128)(2,1)S(1)}, u32[]{:S(2)}, u32[]{:S(2)}) collective-permute-start(bf16[512,512]{1,0:T(8,128)(2,1)S(1)} %collective-permute-done.4.rest_0_.rest_4_), channel_id=1, source_target_pairs={{0,1},{1,0},{2,3},{3,2},{4,5},{5,4},{6,7},{7,6},{8,9},{9,8},{10,11... | collective-permute-start | bytes 1572872 | tf_op jit(solution)/shard_map/ppermute | solution.py:50
  41.9 9.5 %collective-permute-start.6 = (bf16[512,512]{1,0:T(8,128)(2,1)S(1)}, bf16[512,512]{1,0:T(8,128)(2,1)S(1)}, u32[]{:S(2)}, u32[]{:S(2)}) collective-permute-start(bf16[512,512]{1,0:T(8,128)(2,1)S(1)} %collective-permute-done.4.rest_0_.rest_4_), channel_id=1, source_target_pairs={{0,8},{1,3},{2,10},{3,5},{4,12},{5,7},{6,14},{7,1},{8,16},{9,11},{... | collective-permute-start | bytes 1572872 | tf_op jit(solution)/shard_map/ppermute | solution.py:46
  51.5 2.9 %collective-permute-start.10 = (bf16[512,512]{1,0:T(8,128)(2,1)S(1)}, bf16[512,512]{1,0:T(8,128)(2,1)S(1)}, u32[]{:S(2)}, u32[]{:S(2)}) collective-permute-start(bf16[512,512]{1,0:T(8,128)(2,1)S(1)} %collective-permute-done.6.rest_0_), channel_id=1, source_target_pairs={{0,1},{1,0},{2,3},{3,2},{4,5},{5,4},{6,7},{7,6},{8,9},{9,8},{10,11... | collective-permute-start | bytes 1572872 | tf_op jit(solution)/shard_map/ppermute | solution.py:50
